TPU v7x, 256 devices: a whole 4x4x8 slice. The times are simulated.
256 devices in a mesh: lon: 64 (over x, z, y_hi), chan: 4 (over y_lo, core).
Axes of the slice: x: 4, y: 4 (y_hi: 2, y_lo: 2; y = y_hi * 2 + y_lo), z: 8, core: 2. Of those that a mesh axis runs over, the one named last changes fastest.
Arguments:
- coarse: bfloat16 [384, 8, 4096], P('chan', None, 'lon'), may hold values from -6 to 6
- up_weight: bfloat16 [4, 4, 384, 192], replicated, may hold values from -0.15625 to 0.15625
- up_bias: float32 [192], replicated, may hold values from -3 to 3
- conv_weight: bfloat16 [3, 3, 192, 192], replicated, may hold values from -0.15625 to 0.15625
- conv_bias: float32 [192], replicated, may hold values from -3 to 3
- cotangent: bfloat16 [192, 16, 8192], P('chan', None, 'lon'), may hold values from -6 to 6
Outputs:
- refined: bfloat16 [192, 16, 8192], P('chan', None, 'lon')
- coarse_grad: bfloat16 [384, 8, 4096], P('chan', None, 'lon')
- up_grad: float32 [4, 4, 384, 192], P(None, None, 'chan')
- conv_grad: float32 [3, 3, 192, 192], P(None, None, None, 'chan')
All inputs are finite; a program needn't handle non-finite values.
Results may differ from a plain program's by a relative error of at most 0.0049.
Values may be sent and summed in bfloat16 or wider, within the bound.
A program may use at most 64 MiB of HBM per device.

v0:
```python
import jax
import jax.numpy as jnp
from jax import lax
from jax.sharding import PartitionSpec as P

TAPS = (((1, 0), (3, -1)), ((0, 1), (2, 0)))


def with_halo(shard, sides, width):
    for axis, dim in sides:
        size, length = (lax.axis_size(axis), shard.shape[dim])
        up = [(i, (i + 1) % size) for i in range(size)]
        down = [(j, i) for i, j in up]
        last = lax.slice_in_dim(shard, length - width, length, axis=dim)
        initial = lax.slice_in_dim(shard, 0, width, axis=dim)
        before = lax.ppermute(last, axis, up)
        after = lax.ppermute(initial, axis, down)
        shard = jnp.concatenate([before, shard, after], axis=dim)
    return shard


def band_pad(field):
    return jnp.pad(field, ((0, 0), (1, 1), (0, 0)))


def transposed_taps(padded, weight):
    rows = padded.shape[1] - 2
    cols = padded.shape[2] - 2
    parities = []
    for row_par in range(2):
        pair = []
        for col_par in range(2):
            total = None
            for tap_y, row_off in TAPS[row_par]:
                for tap_x, col_off in TAPS[col_par]:
                    window = padded[
                        :, 1 + row_off : 1 + row_off + rows, 1 + col_off : 1 + col_off + cols
                    ]
                    term = jnp.einsum(
                        "chw,co->ohw",
                        window,
                        weight[tap_y, tap_x],
                        preferred_element_type=jnp.float32,
                    )
                    total = term if total is None else total + term
            pair.append(total)
        parities.append(jnp.stack(pair, -1))
    stacked = jnp.stack(parities, 2)
    return stacked.reshape(stacked.shape[0], 2 * rows, 2 * cols)


def cross_taps(padded, weight):
    rows = padded.shape[1] - 2
    cols = padded.shape[2] - 2
    total = None
    for tap_y in range(3):
        for tap_x in range(3):
            window = padded[:, tap_y : tap_y + rows, tap_x : tap_x + cols]
            term = jnp.einsum(
                "chw,co->ohw", window, weight[tap_y, tap_x], preferred_element_type=jnp.float32
            )
            total = term if total is None else total + term
    return total


def cross_adjoint(padded, weight):
    rows = padded.shape[1] - 2
    cols = padded.shape[2] - 2
    total = None
    for tap_y in range(3):
        for tap_x in range(3):
            window = padded[:, 2 - tap_y : 2 - tap_y + rows, 2 - tap_x : 2 - tap_x + cols]
            term = jnp.einsum(
                "ohw,co->chw", window, weight[tap_y, tap_x], preferred_element_type=jnp.float32
            )
            total = term if total is None else total + term
    return total


def cross_weight_grad(padded, grad):
    rows = padded.shape[1] - 2
    cols = padded.shape[2] - 2
    outer = []
    for tap_y in range(3):
        inner = []
        for tap_x in range(3):
            window = padded[:, tap_y : tap_y + rows, tap_x : tap_x + cols]
            inner.append(
                jnp.einsum("chw,ohw->co", window, grad, preferred_element_type=jnp.float32)
            )
        outer.append(jnp.stack(inner, 0))
    return jnp.stack(outer, 0)


def parity_view(padded, tap_y, tap_x):
    rows = (padded.shape[1] - 2) // 2
    cols = (padded.shape[2] - 2) // 2
    split = padded.reshape(padded.shape[0], rows + 1, 2, cols + 1, 2)
    return split[
        :, tap_y // 2 : tap_y // 2 + rows, tap_y % 2, tap_x // 2 : tap_x // 2 + cols, tap_x % 2
    ]


def transposed_weight_grad(coarse, padded_delta):
    outer = []
    for tap_y in range(4):
        inner = []
        for tap_x in range(4):
            view = parity_view(padded_delta, tap_y, tap_x)
            inner.append(
                jnp.einsum("chw,ohw->co", coarse, view, preferred_element_type=jnp.float32)
            )
        outer.append(jnp.stack(inner, 0))
    return jnp.stack(outer, 0)


def transposed_adjoint(padded_delta, weight):
    total = None
    for tap_y in range(4):
        for tap_x in range(4):
            view = parity_view(padded_delta, tap_y, tap_x)
            term = jnp.einsum(
                "ohw,co->chw", view, weight[tap_y, tap_x], preferred_element_type=jnp.float32
            )
            total = term if total is None else total + term
    return total


def local(coarse, up_weight, up_bias, conv_weight, conv_bias, cotangent):
    rank = lax.axis_index("chan")
    cin_dev = coarse.shape[0]
    cout_dev = cotangent.shape[0]
    own_out = rank * cout_dev
    own_in = rank * cin_dev
    up_bias_own = lax.dynamic_slice_in_dim(up_bias, own_out, cout_dev)
    conv_bias_own = lax.dynamic_slice_in_dim(conv_bias, own_out, cout_dev)
    up_in_own = lax.dynamic_slice_in_dim(up_weight, own_in, cin_dev, 2)
    conv_out_own = lax.dynamic_slice_in_dim(conv_weight, own_out, cout_dev, 3)
    coarse_pad = band_pad(with_halo(coarse, (("lon", 2),), 1))
    pre_act = lax.psum_scatter(
        transposed_taps(coarse_pad, up_in_own), "chan", scatter_dimension=0, tiled=True
    )
    pre_act = pre_act + up_bias_own[:, None, None]
    sigma = jax.nn.sigmoid(pre_act)
    hidden = (pre_act * sigma).astype(jnp.bfloat16)
    hidden_every = lax.all_gather(hidden, "chan", axis=0, tiled=True)
    hidden_pad = band_pad(with_halo(hidden_every, (("lon", 2),), 1))
    refined = (cross_taps(hidden_pad, conv_out_own) + conv_bias_own[:, None, None]).astype(
        jnp.bfloat16
    )
    conv_part = cross_weight_grad(hidden_pad, cotangent)
    grad_pad = band_pad(with_halo(cotangent, (("lon", 2),), 1))
    hidden_grad = lax.psum_scatter(
        cross_adjoint(grad_pad, conv_out_own), "chan", scatter_dimension=0, tiled=True
    )
    delta = (hidden_grad * sigma * (1.0 + pre_act * (1.0 - sigma))).astype(jnp.bfloat16)
    delta_every = lax.all_gather(delta, "chan", axis=0, tiled=True)
    delta_pad = band_pad(with_halo(delta_every, (("lon", 2),), 1))
    up_part = transposed_weight_grad(coarse, delta_pad)
    coarse_grad = transposed_adjoint(delta_pad, up_in_own).astype(jnp.bfloat16)
    up_grad, conv_grad = lax.psum((up_part, conv_part), "lon")
    return (refined, coarse_grad, up_grad, conv_grad)


def solution(mesh):
    placed = (P("chan", None, "lon"), P(), P(), P(), P(), P("chan", None, "lon"))
    return jax.shard_map(
        local,
        mesh=mesh,
        in_specs=placed,
        out_specs=(
            P("chan", None, "lon"),
            P("chan", None, "lon"),
            P(None, None, "chan", None),
            P(None, None, None, "chan"),
        ),
        check_vma=False,
    )
```

profile of v0, /device:TPU:8, one launch (start us, length us, event | category | flops | bytes accessed | tf_op | source)
XLA Modules:
  0.0 921.2 jit_solution(13488064533825272959)
XLA Ops:
  8.1 2.4 collective-permute-start
  10.5 7.6 collective-permute-start.1
  20.6 2.0 fusion.106
  29.2 3.0 copy.85
  32.2 3.6 reshape.6
  35.8 2.8 copy.86
  39.6 8.2 collective-permute-start.5
  49.1 2.9 collective-permute-done.4
  61.8 3.0 add_add_fusion
  65.1 26.9 %reduce-scatter.5.cloned.1.call-done = f32[48,16,128]{2,0,1:T(8,128)} async-done(((f32[192,16,128]{2,0,1:T(8,128)}), f32[48,16,128]{2,0,1:T(8,128)}) %reduce-scatter.5.cloned.1.call-update) | async-done | bytes 393232 | tf_op jit(solution)/shard_map/reduce_scatter | solution.py:153
  93.3 8.7 all_gather.6
  103.0 2.0 fusion.96
  105.0 1.4 fusion.177
  106.5 9.1 all_gather.7
  115.5 1.5 copy.87
  117.0 1.5 copy.88
  118.5 7.2 collective-permute-start.3
  125.8 2.8 fusion.176
  128.6 1.5 copy.99
  130.1 1.5 copy.100
  131.6 7.8 collective-permute-start.7
  140.8 2.3 convolution_bitcast_fusion.21
  143.2 2.2 fusion.74
  146.6 2.2 fusion.5
  163.3 1.6 fusion.13
  169.5 3.4 pad_maximum_fusion.1
  172.9 2.8 copy.174
  175.7 2.5 pad.18.clone
  178.2 3.7 reshape.7
  181.9 12.2 %fusion.175 = (bf16[192,8,1,64,1]{0,4,3,2,1:T(2,128)(2,1)S(1)}, bf16[192,8,1,64,1]{0,4,3,2,1:T(2,128)(2,1)S(1)}, bf16[192,8,1,64,1]{0,4,3,2,1:T(2,128)(2,1)S(1)}...) fusion(bf16[192,9,2,65,2]{0,4,3,2,1:T(2,128)(2,1)} %reshape.7), kind=kLoop, calls=%fused_computation.261 | loop fusion | bytes 6291456 | tf_op jit(solution)/shard_map/slice | solution.py:99
  216.7 693.8 %all-reduce.7.cloned.1.call-done = (f32[4,4,96,192]{2,3,1,0:T(8,128)}, f32[3,3,192,48]{2,3,1,0:T(8,128)}) async-done(((f32[4,4,96,192]{2,3,1,0:T(8,128)}, f32[3,3,192,48]{2,3,1,0:T(8,128)}), (f32[4,4,96,192]{2,3,1,0:T(8,128)}, f32[3,3,192,48]{2,3,1,0:T(8,128)})) %all-reduce.7.cloned.1.call-update) | async-done | bytes 1511440 | tf_op jit(solution)/shard_map/psum | solution.py:161
  910.4 3.2 copy.130
  (201 shorter events, 68.6 us)
Async XLA Ops:
  7.2 10.9 %copy-start = (bf16[4,4,384,192]{2,3,1,0:T(8,128)(2,1)S(1)}, bf16[4,4,384,192]{2,3,1,0:T(8,128)(2,1)}, u32[]{:S(2)}) copy-start(bf16[4,4,384,192]{2,3,1,0:T(8,128)(2,1)} %param.7) | copy-start | bytes 7077892
  7.2 15.4 %copy-start.1 = (bf16[96,8,64]{0,2,1:T(8,128)(2,1)S(1)}, bf16[96,8,64]{0,2,1:T(8,128)(2,1)}, u32[]{:S(2)}) copy-start(bf16[96,8,64]{0,2,1:T(8,128)(2,1)} %param.6) | copy-start | bytes 294916
  7.2 57.9 %reduce-scatter.3.cloned.1.call-start = ((), (), s32[]{:S(2)}) async-start(), calls=%async_computation.2 | async-start | bytes 1966080 | tf_op jit(solution)/shard_map/reduce_scatter | solution.py:140
  8.1 15.6 %collective-permute-start = (bf16[96,8,1]{0,2,1:T(2,128)(2,1)S(1)}, bf16[96,8,1]{0,2,1:T(2,128)(2,1)S(1)}, u32[]{:S(2)}, u32[]{:S(2)}) collective-permute-start(bf16[96,8,1]{0,2,1:T(2,128)(2,1)S(1)} %get-tuple-element.50), channel_id=1, source_target_pairs={{0,4},{4,8},{8,12},{12,16},{16,20},{20,24},{24,28},{28,32},{32,36}... | collective-permute-start | bytes 4616 | tf_op jit(solution)/shard_map/ppermute | solution.py:16
  10.5 13.2 %collective-permute-start.1 = (bf16[96,8,1]{0,2,1:T(2,128)(2,1)S(1)}, bf16[96,8,1]{0,2,1:T(2,128)(2,1)S(1)}, u32[]{:S(2)}, u32[]{:S(2)}) collective-permute-start(bf16[96,8,1]{0,2,1:T(2,128)(2,1)S(1)} %get-tuple-element.51), channel_id=1, source_target_pairs={{4,0},{8,4},{12,8},{16,12},{20,16},{24,20},{28,24},{32,28},{36,32}... | collective-permute-start | bytes 4616 | tf_op jit(solution)/shard_map/ppermute | solution.py:17
  35.8 2.9 copy-start.5
  38.7 53.2 %reduce-scatter.5.cloned.1.call-start = ((), (), s32[]{:S(2)}) async-start(), calls=%async_computation.3 | async-start | bytes 1966080 | tf_op jit(solution)/shard_map/reduce_scatter | solution.py:153
  39.6 12.4 %collective-permute-start.4 = (bf16[48,16,1]{2,0,1:T(8,128)(2,1)}, bf16[48,16,1]{2,0,1:T(8,128)(2,1)S(1)}, u32[]{:S(2)}, u32[]{:S(2)}) collective-permute-start(bf16[48,16,1]{2,0,1:T(8,128)(2,1)} %get-tuple-element.40), channel_id=1, source_target_pairs={{0,4},{4,8},{8,12},{12,16},{16,20},{20,24},{24,28},{28,32},{32,36}... | collective-permute-start | bytes 4616 | tf_op jit(solution)/shard_map/ppermute | solution.py:16
  39.6 12.6 %collective-permute-start.5 = (bf16[48,16,1]{2,0,1:T(8,128)(2,1)S(1)}, bf16[48,16,1]{2,0,1:T(8,128)(2,1)S(1)}, u32[]{:S(2)}, u32[]{:S(2)}) collective-permute-start(bf16[48,16,1]{2,0,1:T(8,128)(2,1)S(1)} %get-tuple-element.41), channel_id=1, source_target_pairs={{4,0},{8,4},{12,8},{16,12},{20,16},{24,20},{28,24},{32,28},{36,32}... | collective-permute-start | bytes 4616 | tf_op jit(solution)/shard_map/ppermute | solution.py:17
  61.8 3.1 copy-start.32
  61.8 3.1 copy-start.33
  64.8 845.6 %all-reduce.7.cloned.1.call-start = ((), (), s32[]{:S(2)}) async-start(), calls=%async_computation.4 | async-start | bytes 4030464 | tf_op jit(solution)/shard_map/psum | solution.py:161
  118.5 26.8 %collective-permute-start.3 = (bf16[192,16,1]{0,1,2:T(8,128)(2,1)S(1)}, bf16[192,16,1]{0,1,2:T(8,128)(2,1)S(1)}, u32[]{:S(2)}, u32[]{:S(2)}) collective-permute-start(bf16[192,16,1]{0,1,2:T(8,128)(2,1)S(1)} %copy.88), channel_id=1, source_target_pairs={{4,0},{8,4},{12,8},{16,12},{20,16},{24,20},{28,24},{32,28},{36,32}... | collective-permute-start | bytes 18440 | tf_op jit(solution)/shard_map/ppermute | solution.py:17
  125.8 13.8 %collective-permute-start.2 = (bf16[192,16,1]{0,1,2:T(8,128)(2,1)S(1)}, bf16[192,16,1]{0,1,2:T(8,128)(2,1)S(1)}, u32[]{:S(2)}, u32[]{:S(2)}) collective-permute-start(bf16[192,16,1]{0,1,2:T(8,128)(2,1)S(1)} %copy.87), channel_id=1, source_target_pairs={{0,4},{4,8},{8,12},{12,16},{16,20},{20,24},{24,28},{28,32},{32,36}... | collective-permute-start | bytes 18440 | tf_op jit(solution)/shard_map/ppermute | solution.py:16
  131.6 36.6 %collective-permute-start.7 = (bf16[192,16,1]{0,1,2:T(8,128)(2,1)S(1)}, bf16[192,16,1]{0,1,2:T(8,128)(2,1)S(1)}, u32[]{:S(2)}, u32[]{:S(2)}) collective-permute-start(bf16[192,16,1]{0,1,2:T(8,128)(2,1)S(1)} %copy.100), channel_id=1, source_target_pairs={{4,0},{8,4},{12,8},{16,12},{20,16},{24,20},{28,24},{32,28},{36,32}... | collective-permute-start | bytes 18440 | tf_op jit(solution)/shard_map/ppermute | solution.py:17
  139.4 27.6 %collective-permute-start.6 = (bf16[192,16,1]{0,1,2:T(8,128)(2,1)S(1)}, bf16[192,16,1]{0,1,2:T(8,128)(2,1)S(1)}, u32[]{:S(2)}, u32[]{:S(2)}) collective-permute-start(bf16[192,16,1]{0,1,2:T(8,128)(2,1)S(1)} %copy.99), channel_id=1, source_target_pairs={{0,4},{4,8},{8,12},{12,16},{16,20},{20,24},{24,28},{28,32},{32,36}... | collective-permute-start | bytes 18440 | tf_op jit(solution)/shard_map/ppermute | solution.py:16
  157.7 4.3 copy-start.9
  157.7 4.3 copy-start.10
  160.5 2.8 copy-start.4
  166.2 3.2 copy-start.3
  204.4 6.0 copy-start.23
  204.4 6.0 copy-start.24
  204.4 6.0 copy-start.25
  204.4 6.1 copy-start.29
  204.4 6.1 copy-start.30
  204.4 6.1 copy-start.31
  205.4 5.1 copy-start.26
  205.4 5.1 copy-start.27
  205.5 5.1 copy-start.28
  212.8 2.7 copy-start.11
  212.8 2.7 copy-start.12
  910.4 3.2 copy-start.22
  (13 other events, 30.7 us)
Sparse Core Ops, SparseCore 0:
  38.8 23.3 reduce-scatter.2
  65.3 26.5 reduce-scatter.4
  212.9 697.4 all-reduce.6
where the time goes:
time: 930 us; the launch traced here: 921 us
  waiting for transfers between devices  724 us (78%)
  matrix products  65.3 us (7%)
  local copies, waits for them, and re-layouts  54.1 us (6%)
  starting transfers between devices  33.4 us (4%)
  blocking collectives  17.8 us (2%)
  between operations  15 us (2%)
  other arithmetic  11.7 us (1%)
    psum x1, waiting for transfers between devices, local(): up_grad, conv_grad = lax.psum((up_part, conv_part), 'lon')  694 us
    ppermute x4, starting transfers between devices, with_halo(): after = lax.ppermute(initial, axis, down)  30.8 us
    reduce_scatter x1, waiting for transfers between devices, local(): lax.psum_scatter(cross_adjoint(grad_pad, conv_out_own), 'chan', scatter_d...  26.9 us
    unnamed x32, matrix products  23.1 us
  transfers between devices with their start and end apart: 11, of which 4 were waited for; matrix products, arithmetic and copies ran while one was open for 6% of the time, Pallas kernels for 0%

commit v1 on v0

v1 whole, which is shorter than its diff:
```python
import functools

import jax
import jax.numpy as jnp
from jax import lax
from jax.experimental import pallas as pl
from jax.experimental.pallas import tpu as pltpu
from jax.sharding import PartitionSpec as P

MESH = pl.DeviceIdType.MESH
F32, BF16 = jnp.float32, jnp.bfloat16
VM = pl.BlockSpec(memory_space=pltpu.VMEM)
CIN, COUT, H, WC = 384, 192, 8, 64
OWN_IN, OWN_OUT = CIN // 4, COUT // 4
POS, FINE = H * WC, 4 * H * WC
ROWS = 3072
LIMIT = 60 << 20


def nn(a, b):
    return jnp.dot(a, b, preferred_element_type=F32)


def nt(a, b):
    return lax.dot_general(a, b, (((1,), (1,)), ((), ())), preferred_element_type=F32)


def down(v):
    row = lax.broadcasted_iota(jnp.int32, v.shape, v.ndim - 2)
    return jnp.where(row == 0, 0.0, pltpu.roll(v, 1, v.ndim - 2))


def up(v):
    row = lax.broadcasted_iota(jnp.int32, v.shape, v.ndim - 2)
    return jnp.where(row == H - 1, 0.0, pltpu.roll(v, H - 1, v.ndim - 2))


PIECES = 4


def gather_kernel(coarse, cot, edge, c_all, g_all, e_all, cs, cr, gs, gr, es, er):
    lon, rank = lax.axis_index("lon"), lax.axis_index("chan")
    n_lon = lax.axis_size("lon")
    far, core = rank // 2, lax.rem(rank, 2)
    sib, cross = far * 2 + 1 - core, (1 - far) * 2 + core
    diag = (1 - far) * 2 + 1 - core
    sides = (lax.rem(lon + 1, n_lon), lax.rem(lon + n_lon - 1, n_lon))

    barrier = pltpu.get_barrier_semaphore()
    for d in range(1, 4):
        pl.semaphore_signal(barrier, inc=1, device_id=(lon, lax.rem(rank + d, 4)), device_id_type=MESH)
    for side in sides:
        for d in range(4):
            pl.semaphore_signal(barrier, inc=1, device_id=(side, lax.rem(rank + d, 4)), device_id_type=MESH)
    pl.semaphore_wait(barrier, 11)

    def c_block(r):
        return c_all.at[pl.ds(pl.multiple_of(r * OWN_IN, 16), OWN_IN), :]

    width = FINE // PIECES

    def g_block(r, k):
        return g_all.at[pl.ds(pl.multiple_of(r * OWN_OUT, 16), OWN_OUT), pl.ds(k * width, width)]

    def send(src, dst, s, r, to):
        copy = pltpu.make_async_remote_copy(
            src_ref=src, dst_ref=dst, send_sem=s, recv_sem=r, device_id=to, device_id_type=MESH
        )
        copy.start()
        return copy

    out = []
    c_cross = send(coarse, c_block(rank), cs.at[0], cr.at[0], (lon, cross))
    c_sib = send(coarse, c_block(rank), cs.at[1], cr.at[1], (lon, sib))
    e_copies = []
    for n, side in enumerate(sides):
        for d in range(4):
            to = lax.rem(rank + d, 4)
            dst = e_all.at[n, pl.ds(pl.multiple_of(rank * OWN_OUT, 16), OWN_OUT), :]
            e_copies.append(send(edge, dst, es.at[n, d], er.at[n, d], (side, to)))
    g_cross, g_sib = [], []
    for k in range(PIECES):
        src = cot.at[:, pl.ds(k * width, width)]
        g_cross.append(send(src, g_block(rank, k), gs.at[0, k], gr.at[0, k], (lon, cross)))
        g_sib.append(send(src, g_block(rank, k), gs.at[1, k], gr.at[1, k], (lon, sib)))
    c_all[pl.ds(pl.multiple_of(rank * OWN_IN, 16), OWN_IN), :] = coarse[...]
    g_all[pl.ds(pl.multiple_of(rank * OWN_OUT, 16), OWN_OUT), :] = cot[...]

    def arrival(dst, r):
        return pltpu.make_async_remote_copy(
            src_ref=dst, dst_ref=dst, send_sem=r, recv_sem=r, device_id=(lon, sib), device_id_type=MESH
        )

    arrival(c_block(cross), cr.at[0]).wait_recv()
    out.append(send(c_block(cross), c_block(cross), cs.at[2], cr.at[2], (lon, sib)))
    for k in range(PIECES):
        arrival(g_block(cross, k), gr.at[0, k]).wait_recv()
        out.append(send(g_block(cross, k), g_block(cross, k), gs.at[2, k], gr.at[2, k], (lon, sib)))
    arrival(c_block(sib), cr.at[1]).wait_recv()
    arrival(c_block(diag), cr.at[2]).wait_recv()
    for k in range(PIECES):
        arrival(g_block(sib, k), gr.at[1, k]).wait_recv()
        arrival(g_block(diag, k), gr.at[2, k]).wait_recv()
    for n in range(2):
        for d in range(4):
            origin = lax.rem(rank + 4 - d, 4)
            dst = e_all.at[n, pl.ds(pl.multiple_of(origin * OWN_OUT, 16), OWN_OUT), :]
            arrival(dst, er.at[n, d]).wait_recv()
    for copy in [c_cross, c_sib] + e_copies + g_cross + g_sib + out:
        copy.wait_send()


def gather(coarse, cot, edge):
    dma = pltpu.SemaphoreType.DMA
    return pl.pallas_call(
        gather_kernel,
        out_shape=(
            jax.ShapeDtypeStruct((CIN, POS), BF16),
            jax.ShapeDtypeStruct((COUT, FINE), BF16),
            jax.ShapeDtypeStruct((2, COUT, 128), BF16),
        ),
        in_specs=[VM] * 3,
        out_specs=[VM] * 3,
        scratch_shapes=[
            dma((3,)), dma((3,)), dma((3, PIECES)), dma((3, PIECES)), dma((2, 4)), dma((2, 4)),
        ],
        compiler_params=pltpu.CompilerParams(collective_id=0, has_side_effects=True),
        name="gather",
    )(coarse, cot, edge)


def compute_kernel(rank_ref, c_all, g_all, e_all, coarse, cot, up_w, up_b, conv_w, conv_b,
                   refined, c_grad, packed, xf, xl, pre, fs, hid, cots, df):
    rank = rank_ref[0]

    for b in range(4):
        xf[pl.ds(1 + 16 * b, 16)] = c_all[:, pl.ds(128 * b, 128)].astype(F32).T.reshape(16, H, CIN)
    left, right = e_all[0].astype(F32).T, e_all[1].astype(F32).T
    src = lax.broadcasted_iota(jnp.int32, (COUT, CIN), 0)
    dst = lax.broadcasted_iota(jnp.int32, (COUT, CIN), 1)
    place = src // OWN_OUT * OWN_IN + lax.rem(src, OWN_OUT)
    spread = [(dst == place + OWN_OUT * h).astype(F32).astype(BF16) for h in range(2)]

    def widen(pair):
        return nn(pair[:16].astype(BF16), spread[0]) + nn(pair[16:].astype(BF16), spread[1])

    xf[0] = widen(left[96:128])[8:]
    xf[65] = widen(right[32:64])[:8]
    xf[66:68] = jnp.zeros((2, H, CIN), F32)

    @pl.loop(0, 3)
    def _(n):
        t0 = n * 22
        rows = pl.ds(pl.multiple_of(t0 * H, 16), 22 * H)
        for d in range(2):
            v = xf[pl.ds(t0 + 1 - d, 22)]
            for s, w in enumerate((down(v), v, up(v))):
                xl[rows, pl.ds((2 * s + d) * CIN, CIN)] = w.reshape(22 * H, CIN).astype(BF16)

    for rp in range(2):
        for cp in range(2):
            taps = ((3, 1), (2, 0))[rp]
            w = jnp.concatenate([up_w[ky, cp + 2 * d] for ky in taps for d in range(2)], 0)
            val = nn(xl[:, pl.ds(rp * 2 * CIN, 4 * CIN)], w)
            pre[:, cp, rp] = val.reshape(66, H, COUT)

    bias = up_b[...].reshape(1, 1, 1, 1, COUT)

    @pl.loop(0, 22)
    def _(n):
        ts = pl.ds(n * 3, 3)
        z = pre[ts] + bias
        s = jax.nn.sigmoid(z)
        fs[ts] = s * (1.0 + z * (1.0 - s))
        h = (z * s).astype(BF16).astype(F32)
        even, odd = h[:, :, 0], h[:, :, 1]
        for m, (a, b) in enumerate(((down(odd), even), (even, odd), (odd, up(even)))):
            both = jnp.concatenate([a, b], 2).astype(BF16)
            hid[m, pl.ds(n * 6, 6)] = both.reshape(6, 16, COUT)

    def put(at, v, n):
        v = v.reshape(n, 2, H, COUT)
        even, odd = v[:, 0], v[:, 1]
        for m, (a, b) in enumerate(((down(odd), even), (even, odd), (odd, up(even)))):
            cots[m, pl.ds(at, n)] = jnp.concatenate([a, b], 1).astype(BF16)

    put(0, left[64:96], 2)
    put(130, right[0:32], 2)
    for b in range(16):
        put(2 + 8 * b, g_all[:, pl.ds(128 * b, 128)].astype(F32).T, 8)

    @pl.loop(0, 5)
    def _(n):
        acc = None
        for ky in range(3):
            for kx in range(3):
                g = cots[2 - ky, pl.ds(n * 26 + 2 - kx, 26)].reshape(416, COUT)
                term = nt(g, conv_w[ky, kx])
                acc = term if acc is None else acc + term
        ts = pl.ds(n * 13, 13)
        d = (acc.reshape(13, 2, 2, H, COUT) * fs[ts]).astype(BF16).astype(F32)
        for cp in range(2):
            even, odd = d[:, cp, 0], d[:, cp, 1]
            for ky, v in enumerate((down(odd), even, odd, up(even))):
                df[cp, ky, ts] = v

    own = pl.ds(pl.multiple_of(rank * OWN_IN, 16), OWN_IN)
    total = None
    for ky in range(4):
        for pair in range(2):
            ab = []
            for kx in (2 * pair, 2 * pair + 1):
                w = df[kx % 2, ky, pl.ds(kx // 2, 64)].reshape(POS, COUT).astype(BF16)
                ab.append(nn(coarse[...], w))
                term = nt(up_w[ky, kx, own, :], w)
                total = term if total is None else total + term
            a, b = ab
            base = ky * 768 + pair * 288
            packed[pl.ds(base, 96), :] = a[:, :128].astype(BF16)
            packed[pl.ds(base + 96, 96), :] = jnp.concatenate([a[:, 128:], b[:, :64]], 1).astype(BF16)
            packed[pl.ds(base + 192, 96), :] = b[:, 64:].astype(BF16)
    c_grad[...] = total.astype(BF16)

    k_of = lax.broadcasted_iota(jnp.int32, (OWN_OUT, COUT), 0)
    o_of = lax.broadcasted_iota(jnp.int32, (OWN_OUT, COUT), 1)
    pick = (o_of == k_of + OWN_OUT * rank).astype(F32).astype(BF16)
    mine = [nt(pick, conv_w[t // 3, t % 3]).astype(BF16) for t in range(9)]

    for n in range(8):
        acc = None
        for t in range(9):
            term = nt(mine[t], hid[t // 3, pl.ds(16 * n + t % 3, 16)].reshape(256, COUT))
            acc = term if acc is None else acc + term
        refined[:, pl.ds(256 * n, 256)] = (acc + conv_b[...]).astype(BF16)

    def spot(b):
        return pl.ds(b // 4 * 768 + 576 + b % 4 * OWN_OUT, OWN_OUT)

    tails = []
    for t in range(9):
        g = nn(cot[...], hid[t // 3, pl.ds(t % 3, 128)].reshape(FINE, COUT))
        packed[spot(t), :] = g[:, :128].astype(BF16)
        tails.append(g[:, 128:])
    tails.append(jnp.zeros((OWN_OUT, 64), F32))
    for u in range(5):
        packed[spot(9 + u), :] = jnp.concatenate(tails[2 * u:2 * u + 2], 1).astype(BF16)
    for b in (14, 15):
        packed[spot(b), :] = jnp.zeros((OWN_OUT, 128), BF16)


def compute(rank, *args):
    return pl.pallas_call(
        compute_kernel,
        out_shape=(
            jax.ShapeDtypeStruct((OWN_OUT, FINE), BF16),
            jax.ShapeDtypeStruct((OWN_IN, POS), BF16),
            jax.ShapeDtypeStruct((ROWS, 128), BF16),
        ),
        in_specs=[pl.BlockSpec(memory_space=pltpu.SMEM)] + [VM] * 9,
        out_specs=[VM] * 3,
        scratch_shapes=[
            pltpu.VMEM((68, H, CIN), F32),
            pltpu.VMEM((528, 6 * CIN), BF16),
            pltpu.VMEM((66, 2, 2, H, COUT), F32),
            pltpu.VMEM((66, 2, 2, H, COUT), F32),
            pltpu.VMEM((3, 132, 16, COUT), BF16),
            pltpu.VMEM((3, 132, 16, COUT), BF16),
            pltpu.VMEM((2, 4, 66, H, COUT), F32),
        ],
        compiler_params=pltpu.CompilerParams(vmem_limit_bytes=LIMIT),
        name="strip",
    )(rank, *args)


def sum_kernel(dims, src, res, rx, sb, rz, ys, yr,
               x_s, x_r, z_s, z_r, y_sem, az_s, az_r, ax_s, ax_r):
    nx, nz, ny = dims
    size = ROWS // (nx * nz)
    lon, rank = lax.axis_index("lon"), lax.axis_index("chan")
    x, z, y = lon // (nz * ny), lax.rem(lon // ny, nz), lax.rem(lon, ny)

    def dev(px, pz, py):
        return ((px * nz + pz) * ny + py, rank)

    xs = [dev(lax.rem(x + d, nx), z, y) for d in range(1, nx)]
    zs = [dev(x, lax.rem(z + d, nz), y) for d in range(1, nz)]
    ypeer = [dev(x, z, 1 - y)] if ny == 2 else []
    barrier = pltpu.get_barrier_semaphore()
    for peer in xs + zs + ypeer:
        pl.semaphore_signal(barrier, inc=1, device_id=peer, device_id_type=MESH)
    pl.semaphore_wait(barrier, len(xs + zs + ypeer))

    def piece(px, pz):
        return pl.ds(pl.multiple_of((px * nz + pz) * size, 16), size)

    started = []

    def copy_of(a, b, s, r, to):
        return pltpu.make_async_remote_copy(
            src_ref=a, dst_ref=b, send_sem=s, recv_sem=r, device_id=to, device_id_type=MESH
        )

    def send(a, b, s, r, to):
        copy = copy_of(a, b, s, r, to)
        copy.start()
        started.append(copy)

    for k in range(nz):
        zz = lax.rem(z + 1 + k, nz)
        for d in range(1, nx):
            px = lax.rem(x + d, nx)
            send(src.at[piece(px, zz), :], rx.at[d - 1, k], x_s.at[d - 1, k], x_r.at[d - 1, k], xs[d - 1])
    acc = None
    for k in range(nz):
        zz = lax.rem(z + 1 + k, nz)
        acc = src[piece(x, zz), :].astype(F32)
        for d in range(1, nx):
            copy_of(rx.at[d - 1, k], rx.at[d - 1, k], x_s.at[d - 1, k], x_r.at[d - 1, k], xs[0]).wait_recv()
            acc = acc + rx[d - 1, k].astype(F32)
        if k < nz - 1:
            sb[k] = acc.astype(BF16)
            send(sb.at[k], rz.at[k], z_s.at[k], z_r.at[k], zs[k])
    for k in range(nz - 1):
        copy_of(rz.at[k], rz.at[k], z_s.at[k], z_r.at[k], zs[0]).wait_recv()
        acc = acc + rz[k].astype(F32)
    if ny == 2:
        ys[...] = acc
        send(ys, yr, y_sem.at[0], y_sem.at[1], ypeer[0])
        copy_of(yr, yr, y_sem.at[0], y_sem.at[1], ypeer[0]).wait_recv()
        acc = acc + yr[...]
    res[piece(x, z), :] = acc.astype(BF16)
    here = res.at[piece(x, z), :]
    for k in range(1, nz):
        send(here, here, az_s.at[k - 1], az_r.at[k - 1], zs[k - 1])
    for k in range(nz):
        part = res.at[piece(x, lax.rem(z + nz - k, nz)), :]
        if k > 0:
            copy_of(part, part, az_s.at[k - 1], az_r.at[k - 1], zs[0]).wait_recv()
        for d in range(1, nx):
            send(part, part, ax_s.at[d - 1, k], ax_r.at[d - 1, k], xs[d - 1])
    for k in range(nz):
        for d in range(1, nx):
            part = res.at[piece(lax.rem(x + nx - d, nx), lax.rem(z + nz - k, nz)), :]
            copy_of(part, part, ax_s.at[d - 1, k], ax_r.at[d - 1, k], xs[0]).wait_recv()
    for copy in started:
        copy.wait_send()


def sum_lon(dims, packed):
    nx, nz, ny = dims
    size = ROWS // (nx * nz)
    dma = pltpu.SemaphoreType.DMA
    return pl.pallas_call(
        functools.partial(sum_kernel, dims),
        out_shape=jax.ShapeDtypeStruct((ROWS, 128), BF16),
        in_specs=[VM],
        out_specs=VM,
        scratch_shapes=[
            pltpu.VMEM((nx - 1, nz, size, 128), BF16),
            pltpu.VMEM((nz - 1, size, 128), BF16),
            pltpu.VMEM((nz - 1, size, 128), BF16),
            pltpu.VMEM((size, 128), F32),
            pltpu.VMEM((size, 128), F32),
            dma((nx - 1, nz)), dma((nx - 1, nz)), dma((nz - 1,)), dma((nz - 1,)), dma((2,)),
            dma((nz - 1,)), dma((nz - 1,)), dma((nx - 1, nz)), dma((nx - 1, nz)),
        ],
        compiler_params=pltpu.CompilerParams(collective_id=1, has_side_effects=True),
        name="sum_lon",
    )(packed)


def unpack_kernel(src, up_grad, conv_grad):
    for ky in range(4):
        for pair in range(2):
            base = ky * 768 + pair * 288
            a, m, b = [src[pl.ds(base + 96 * n, 96), :].astype(F32) for n in range(3)]
            up_grad[ky, 2 * pair] = jnp.concatenate([a, m[:, :64]], 1)
            up_grad[ky, 2 * pair + 1] = jnp.concatenate([m[:, 64:], b], 1)

    def block(b):
        return src[pl.ds(b // 4 * 768 + 576 + b % 4 * OWN_OUT, OWN_OUT), :].astype(F32)

    for t in range(9):
        tail = block(9 + t // 2)[:, 64 * (t % 2):64 * (t % 2) + 64]
        conv_grad[t // 3, t % 3] = jnp.concatenate([block(t), tail], 1).T


def unpack(sums):
    return pl.pallas_call(
        unpack_kernel,
        out_shape=(
            jax.ShapeDtypeStruct((4, 4, OWN_IN, COUT), F32),
            jax.ShapeDtypeStruct((3, 3, COUT, OWN_OUT), F32),
        ),
        in_specs=[VM],
        out_specs=[VM] * 2,
        compiler_params=pltpu.CompilerParams(vmem_limit_bytes=LIMIT),
        name="unpack",
    )(sums)


def local(dims, coarse, up_weight, up_bias, conv_weight, conv_bias, cotangent):
    rank = lax.axis_index("chan")
    conv_b = lax.dynamic_slice_in_dim(conv_bias, rank * OWN_OUT, OWN_OUT).reshape(OWN_OUT, 1)
    c = coarse.transpose(0, 2, 1).reshape(OWN_IN, POS)
    g = cotangent.reshape(OWN_OUT, H, 2, 2 * WC).transpose(0, 3, 2, 1).reshape(OWN_OUT, FINE)
    edge = jnp.concatenate(
        [g[:, :32], c[:48, :16], c[48:, :16], g[:, -32:], c[:48, -16:], c[48:, -16:]], 1
    )
    c_all, g_all, e_all = gather(c, g, edge)
    ref, cg, packed = compute(
        rank.astype(jnp.int32).reshape(1), c_all, g_all, e_all, c, g,
        up_weight, up_bias.reshape(1, COUT), conv_weight, conv_b,
    )
    up_grad, conv_grad = unpack(sum_lon(dims, packed))
    refined = ref.reshape(OWN_OUT, 2 * WC, 2, H).transpose(0, 3, 2, 1).reshape(OWN_OUT, 2 * H, 2 * WC)
    coarse_grad = cg.reshape(OWN_IN, WC, H).transpose(0, 2, 1)
    return refined, coarse_grad, up_grad, conv_grad


def solution(mesh):
    dims = {64: (4, 8, 2), 8: (2, 2, 2), 4: (2, 2, 1)}[mesh.shape["lon"]]
    placed = (P("chan", None, "lon"), P(), P(), P(), P(), P("chan", None, "lon"))
    return jax.shard_map(
        functools.partial(local, dims),
        mesh=mesh,
        in_specs=placed,
        out_specs=(
            P("chan", None, "lon"),
            P("chan", None, "lon"),
            P(None, None, "chan", None),
            P(None, None, None, "chan"),
        ),
        check_vma=False,
    )
```

time: 930 us -> 92 us (0.10)
  the two profiles are of different devices: /device:TPU:8 before, /device:TPU:2 now
where the time goes in v1:
time: 92 us; the launch traced here: 90.7 us
  Pallas kernels  75.7 us (82%)
  local copies, waits for them, and re-layouts  14.3 us (16%)
    pallas_call x1, Pallas kernels, sum_lon(): pl.pallas_call(functools.partial(sum_kernel, dims), out_shape=jax.ShapeDt...  35.7 us
    pallas_call x1, Pallas kernels, gather(): pl.pallas_call(gather_kernel, out_shape=(jax.ShapeDtypeStruct((CIN, POS),...  20.3 us
    pallas_call x1, Pallas kernels, compute(): pl.pallas_call(compute_kernel, out_shape=(jax.ShapeDtypeStruct((OWN_OUT,...  16.8 us
    unnamed x12, local copies, waits for them, and re-layouts  7.19 us
    pallas_call x1, Pallas kernels, unpack(): pl.pallas_call(unpack_kernel, out_shape=(jax.ShapeDtypeStruct((4, 4, OWN_...  2.92 us
    pallas_call x2, local copies, waits for them, and re-layouts, compute(): pl.pallas_call(compute_kernel, out_shape=(jax.ShapeDtypeStruct((OWN_OUT,...  2.22 us

profile of v1, /device:TPU:2, one launch (start us, length us, event | category | flops | bytes accessed | tf_op | source)
XLA Modules:
  0.0 90.7 jit_solution(3261811380731298134)
XLA Ops:
  0.6 0.0 copy-start
  0.6 0.0 copy-start.1
  0.7 0.7 copy-done
  1.3 0.1 dynamic-slice_bitcast_fusion
  1.4 0.7 copy.48.conv_b
  2.1 1.0 %copy.56 = bf16[96,64,8]{0,2,1:T(8,128)(2,1)S(1)} copy(bf16[96,64,8]{0,1,2:T(8,128)(2,1)} %bitcast.25) | data formatting | bytes 196608 | tf_op jit(solution)/shard_map/transpose | solution.py:405
  3.1 0.1 copy.43.coarse
  3.2 0.0 copy-start.3
  3.2 0.1 fusion.1
  3.3 1.5 %copy.36 = bf16[48,8,2,128]{0,1,2,3:T(8,128)(2,1)S(1)} copy(bf16[48,8,2,128]{3,2,1,0:T(2,128)(2,1)} %bitcast.24) | data formatting | bytes 393216 | tf_op jit(solution)/shard_map/reshape | solution.py:406
  4.8 0.2 copy.44.cot
  5.0 0.0 copy-start.2
  5.0 0.1 fusion
  5.1 0.7 concatenate.3.edge
  5.8 0.0 copy-done.3
  5.8 0.0 copy-done.2
  5.8 20.3 %gather.1 = (bf16[384,512]{1,0:T(8,128)(2,1)}, bf16[192,2048]{1,0:T(8,128)(2,1)}, bf16[2,192,128]{2,1,0:T(8,128)(2,1)}) custom-call(bf16[96,512]{1,0:T(8,128)(2,1)} %copy-done.3, bf16[48,2048]{1,0:T(8,128)(2,1)} %copy-done.2, bf16[48,128]{1,0:T(8,128)(2,1)} %concatenate.3.edge), custom_call_target="tpu_custom_call" | custom-call | tf_op jit(solution)/shard_map/gather/pallas_call | solution.py:115
  26.1 0.0 copy-done.1
  26.1 2.8 %copy.47.up_w = bf16[4,4,384,192]{3,2,1,0:T(8,128)(2,1)} copy(bf16[4,4,384,192]{2,3,1,0:T(8,128)(2,1)S(1)} %copy-done.1) | data formatting | bytes 4718592 | tf_op args[1]
  28.9 16.8 %strip.1 = (bf16[48,2048]{1,0:T(8,128)(2,1)}, bf16[96,512]{1,0:T(8,128)(2,1)}, bf16[3072,128]{1,0:T(8,128)(2,1)}) custom-call(s32[1]{0:T(128)} %bitcast.rank_ref, bf16[384,512]{1,0:T(8,128)(2,1)} %get-tuple-element.12.c_all, bf16[192,2048]{1,0:T(8,128)(2,1)} %get-tuple-element.13.g_all, bf16[2,192,128]{2,1,0:T(8,128)(2,1)} %get-tuple-element.14.e_all, ...), custom_call_target="tpu_custom_call" | custom-call | tf_op jit(solution)/shard_map/strip/pallas_call | solution.py:252
  45.7 1.0 %copy.51 = bf16[96,512]{0,1:T(8,128)(2,1)S(1)} copy(bf16[96,512]{1,0:T(8,128)(2,1)} %get-tuple-element.16) | data formatting | bytes 196608 | tf_op jit(solution)/shard_map/strip/pallas_call | solution.py:252
  46.8 0.7 copy.53
  47.4 1.2 %copy.49 = bf16[48,2048]{0,1:T(8,128)(2,1)S(1)} copy(bf16[48,2048]{1,0:T(8,128)(2,1)} %get-tuple-element.15) | data formatting | bytes 393216 | tf_op jit(solution)/shard_map/strip/pallas_call | solution.py:252
  48.7 0.5 copy.50
  49.1 0.7 copy.52
  49.8 35.7 %sum_lon.1.src = bf16[3072,128]{1,0:T(8,128)(2,1)} custom-call(bf16[3072,128]{1,0:T(8,128)(2,1)} %get-tuple-element.17.src), custom_call_target="tpu_custom_call" | custom-call | tf_op jit(solution)/shard_map/sum_lon/pallas_call | solution.py:353
  85.5 2.9 %unpack.1 = (f32[4,4,96,192]{3,2,1,0:T(8,128)}, f32[3,3,192,48]{3,2,1,0:T(8,128)}) custom-call(bf16[3072,128]{1,0:T(8,128)(2,1)} %sum_lon.1.src), custom_call_target="tpu_custom_call" | custom-call | tf_op jit(solution)/shard_map/unpack/pallas_call | solution.py:389
  88.4 2.3 %copy.54 = f32[3,3,192,48]{2,3,1,0:T(8,128)} copy(f32[3,3,192,48]{3,2,1,0:T(8,128)} %get-tuple-element.31) | data formatting | bytes 663552
Async XLA Ops:
  0.6 0.7 copy-start
  0.6 25.5 %copy-start.1 = (bf16[4,4,384,192]{2,3,1,0:T(8,128)(2,1)S(1)}, bf16[4,4,384,192]{2,3,1,0:T(8,128)(2,1)}, u32[]{:S(2)}) copy-start(bf16[4,4,384,192]{2,3,1,0:T(8,128)(2,1)} %param.7) | copy-start | bytes 7077892
  3.2 2.6 %copy-start.3 = (bf16[96,512]{1,0:T(8,128)(2,1)}, bf16[96,512]{1,0:T(8,128)(2,1)S(1)}, u32[]{:S(2)}) copy-start(bf16[96,512]{1,0:T(8,128)(2,1)S(1)} %copy.43.coarse) | copy-start | bytes 294916
  5.0 0.8 copy-start.2

commit v2 on v1

v2 whole, which is shorter than its diff:
```python
import functools

import jax
import jax.numpy as jnp
from jax import lax
from jax.experimental import pallas as pl
from jax.experimental.pallas import tpu as pltpu
from jax.sharding import PartitionSpec as P

MESH = pl.DeviceIdType.MESH
F32, BF16 = jnp.float32, jnp.bfloat16
VM = pl.BlockSpec(memory_space=pltpu.VMEM)
CIN, COUT, H, WC = 384, 192, 8, 64
OWN_IN, OWN_OUT = CIN // 4, COUT // 4
POS, FINE = H * WC, 4 * H * WC
PIECE = 96
LIMIT = 60 << 20


def nn(a, b):
    return jnp.dot(a, b, preferred_element_type=F32)


def nt(a, b):
    return lax.dot_general(a, b, (((1,), (1,)), ((), ())), preferred_element_type=F32)


def down(v):
    row = lax.broadcasted_iota(jnp.int32, v.shape, v.ndim - 2)
    return jnp.where(row == 0, 0.0, pltpu.roll(v, 1, v.ndim - 2))


def up(v):
    row = lax.broadcasted_iota(jnp.int32, v.shape, v.ndim - 2)
    return jnp.where(row == H - 1, 0.0, pltpu.roll(v, H - 1, v.ndim - 2))


PIECES = 4


def shifted(v):
    even, odd = v[:, 0], v[:, 1]
    pairs = ((down(odd), even), (even, odd), (odd, up(even)))
    return [jnp.concatenate(pair, 1).astype(BF16) for pair in pairs]


def kernel(dims, coarse, cot, edge, up_hbm, conv_hbm, up_b, conv_b,
           refined, c_grad, res,
           c_all, g_all, e_all, up_w, conv_w, conv_t, mine, own_up,
           xf, xl, pre, fs, hid, cots, df, part, r_pos, c_pos,
           rx1, kept, sb1, rx2, sb2, rz, ys, yr,
           w_sem, cs, cr, gs, gr, es, er, x1s, x1r, x2s, x2r, zs_s, zs_r, y_sem,
           azs, azr, axs, axr):
    nx, nz, ny = dims
    lon, rank = lax.axis_index("lon"), lax.axis_index("chan")
    n_lon = nx * nz * ny
    x, z, y = lon // (nz * ny), lax.rem(lon // ny, nz), lax.rem(lon, ny)
    far, core = rank // 2, lax.rem(rank, 2)
    sib, cross = far * 2 + 1 - core, (1 - far) * 2 + core
    diag = (1 - far) * 2 + 1 - core
    sides = (lax.rem(lon + 1, n_lon), lax.rem(lon + n_lon - 1, n_lon))
    xa, xb = x + 1 - 2 * lax.rem(x, 2), 3 - x
    xo = lax.rem(x + 2, 4)

    def dev(px, pz, py):
        return ((px * nz + pz) * ny + py, rank)

    def first(zz):
        return xa + lax.rem(zz, 2) * (xb - xa)

    def second(zz):
        return xb + lax.rem(zz, 2) * (xa - xb)

    zpeers = [dev(x, lax.rem(z + d, nz), y) for d in range(1, nz)]
    ypeers = [dev(x, z, 1 - y)] if ny == 2 else []

    loads = [
        pltpu.make_async_copy(up_hbm, up_w, w_sem.at[0]),
        pltpu.make_async_copy(conv_hbm, conv_w, w_sem.at[1]),
    ]
    for load in loads:
        load.start()

    barrier = pltpu.get_barrier_semaphore()
    greet = [(lon, lax.rem(rank + d, 4)) for d in range(1, 4)]
    greet += [(side, lax.rem(rank + d, 4)) for side in sides for d in range(4)]
    greet += [dev(xa, z, y), dev(xb, z, y)] + zpeers + ypeers
    for peer in greet:
        pl.semaphore_signal(barrier, inc=1, device_id=peer, device_id_type=MESH)
    pl.semaphore_wait(barrier, len(greet))

    started = []

    def copy_of(a, b, s, r, to):
        return pltpu.make_async_remote_copy(
            src_ref=a, dst_ref=b, send_sem=s, recv_sem=r, device_id=to, device_id_type=MESH
        )

    def send(a, b, s, r, to):
        copy = copy_of(a, b, s, r, to)
        copy.start()
        started.append(copy)

    def arrived(b, r):
        copy_of(b, b, r, r, (lon, sib)).wait_recv()

    def c_block(r):
        return c_all.at[pl.ds(pl.multiple_of(r * OWN_IN, 16), OWN_IN), :]

    width = FINE // PIECES

    def g_block(r, k):
        return g_all.at[pl.ds(pl.multiple_of(r * OWN_OUT, 16), OWN_OUT), pl.ds(k * width, width)]

    def e_block(n, r):
        return e_all.at[n, pl.ds(pl.multiple_of(r * OWN_OUT, 16), OWN_OUT), :]

    send(coarse, c_block(rank), cs.at[0], cr.at[0], (lon, cross))
    send(coarse, c_block(rank), cs.at[1], cr.at[1], (lon, sib))
    for n, side in enumerate(sides):
        for d in range(4):
            send(edge, e_block(n, rank), es.at[n, d], er.at[n, d], (side, lax.rem(rank + d, 4)))
    for k in range(PIECES):
        own_part = cot.at[:, pl.ds(k * width, width)]
        send(own_part, g_block(rank, k), gs.at[0, k], gr.at[0, k], (lon, cross))
        send(own_part, g_block(rank, k), gs.at[1, k], gr.at[1, k], (lon, sib))
    c_all[pl.ds(pl.multiple_of(rank * OWN_IN, 16), OWN_IN), :] = coarse[...]
    g_all[pl.ds(pl.multiple_of(rank * OWN_OUT, 16), OWN_OUT), :] = cot[...]

    def pass_on(k):
        arrived(g_block(cross, k), gr.at[0, k])
        send(g_block(cross, k), g_block(cross, k), gs.at[2, k], gr.at[2, k], (lon, sib))

    for load in loads:
        load.wait()
    a_of = lax.broadcasted_iota(jnp.int32, (COUT, OWN_OUT), 0)
    b_of = lax.broadcasted_iota(jnp.int32, (COUT, OWN_OUT), 1)
    pick = (a_of == b_of + OWN_OUT * rank).astype(F32).astype(BF16)
    for t in range(9):
        w = conv_w[t // 3, t % 3]
        mine[t] = nn(w, pick).astype(BF16)
        conv_t[t] = w.astype(F32).T.astype(BF16)
    src = lax.broadcasted_iota(jnp.int32, (COUT, CIN), 0)
    dst = lax.broadcasted_iota(jnp.int32, (COUT, CIN), 1)
    place = src // OWN_OUT * OWN_IN + lax.rem(src, OWN_OUT)
    spread = [(dst == place + OWN_OUT * h).astype(F32).astype(BF16) for h in range(2)]

    arrived(c_block(cross), cr.at[0])
    send(c_block(cross), c_block(cross), cs.at[2], cr.at[2], (lon, sib))
    a_of = lax.broadcasted_iota(jnp.int32, (CIN, OWN_IN), 0)
    b_of = lax.broadcasted_iota(jnp.int32, (CIN, OWN_IN), 1)
    pick = (a_of == b_of + OWN_IN * rank).astype(F32).astype(BF16)
    for t in range(16):
        own_up[t] = nn(up_w[t // 4, t % 4], pick).astype(BF16)
    for n in range(2):
        for d in range(4):
            arrived(e_block(n, lax.rem(rank + 4 - d, 4)), er.at[n, d])
    arrived(c_block(sib), cr.at[1])
    arrived(c_block(diag), cr.at[2])
    for b in range(4):
        xf[pl.ds(1 + 16 * b, 16)] = c_all[:, pl.ds(128 * b, 128)].astype(F32).T.reshape(16, H, CIN)
    left, right = e_all[0].astype(F32).T, e_all[1].astype(F32).T

    def widen(pair):
        return nn(pair[:16].astype(BF16), spread[0]) + nn(pair[16:].astype(BF16), spread[1])

    xf[0] = widen(left[96:128])[8:]
    xf[65] = widen(right[32:64])[:8]
    xf[66:68] = jnp.zeros((2, H, CIN), F32)

    @pl.loop(0, 3)
    def _(n):
        t0 = n * 22
        rows = pl.ds(pl.multiple_of(t0 * H, 16), 22 * H)
        for d in range(2):
            v = xf[pl.ds(t0 + 1 - d, 22)]
            for s, w in enumerate((down(v), v, up(v))):
                xl[rows, pl.ds((2 * s + d) * CIN, CIN)] = w.reshape(22 * H, CIN).astype(BF16)

    pass_on(0)
    for rp in range(2):
        for cp in range(2):
            taps = ((3, 1), (2, 0))[rp]
            w = jnp.concatenate([up_w[ky, cp + 2 * d] for ky in taps for d in range(2)], 1)
            val = nt(xl[:, pl.ds(rp * 2 * CIN, 4 * CIN)], w)
            pre[:, cp, rp] = val.reshape(66, H, COUT)
        pass_on(1 + rp)

    bias = up_b[...].reshape(1, 1, 1, 1, COUT)

    @pl.loop(0, 22)
    def _(n):
        ts = pl.ds(n * 3, 3)
        v = pre[ts] + bias
        s = jax.nn.sigmoid(v)
        fs[ts] = s * (1.0 + v * (1.0 - s))
        h = (v * s).astype(BF16).astype(F32).reshape(6, 2, H, COUT)
        for m, w in enumerate(shifted(h)):
            hid[m, pl.ds(n * 6, 6)] = w

    pass_on(3)

    def along_x(chunk, p, which):
        send(part.at[chunk, p], rx1.at[p, which], x1s.at[p, which], x1r.at[p, which],
             dev(first(p), z, y))

    def spot(b):
        return b // 4, 6 + b % 4 // 2, pl.ds(b % 2 * OWN_OUT, OWN_OUT)

    def put(b, v):
        c, p, rows = spot(b)
        part[c, p, rows, :] = v.astype(BF16)

    tails = []
    for t in range(9):
        g = nn(cot[...], hid[t // 3, pl.ds(t % 3, 128)].reshape(FINE, COUT))
        put(t, g[:, :128])
        tails.append(g[:, 128:])
    tails.append(jnp.zeros((OWN_OUT, 64), F32))
    for u in range(5):
        put(9 + u, jnp.concatenate(tails[2 * u:2 * u + 2], 1))
    for b in (14, 15):
        put(b, jnp.zeros((OWN_OUT, 128), F32))
    for p in (6, 7):
        along_x(xo, p, 1)
        along_x(first(p), p, 0)

    for k in range(PIECES):
        arrived(g_block(sib, k), gr.at[1, k])
        arrived(g_block(diag, k), gr.at[2, k])

    def place_cot(at, v, n):
        for m, w in enumerate(shifted(v.reshape(n, 2, H, COUT))):
            cots[m, pl.ds(at, n)] = w

    place_cot(0, left[64:96], 2)
    place_cot(130, right[0:32], 2)
    for b in range(16):
        place_cot(2 + 8 * b, g_all[:, pl.ds(128 * b, 128)].astype(F32).T, 8)

    @pl.loop(0, 5)
    def _(n):
        acc = None
        for ky in range(3):
            for kx in range(3):
                g = cots[2 - ky, pl.ds(n * 26 + 2 - kx, 26)].reshape(416, COUT)
                term = nn(g, conv_t[ky * 3 + kx])
                acc = term if acc is None else acc + term
        ts = pl.ds(n * 13, 13)
        d = (acc.reshape(13, 2, 2, H, COUT) * fs[ts]).astype(BF16).astype(F32)
        for cp in range(2):
            even, odd = d[:, cp, 0], d[:, cp, 1]
            for ky, v in enumerate((down(odd), even, odd, up(even))):
                df[cp, ky, ts] = v

    def window(ky, kx):
        return df[kx % 2, ky, pl.ds(kx // 2, 64)].reshape(POS, COUT).astype(BF16)

    for ky in (xo, xa, xb, x):
        for pair in range(2):
            a, b = [nn(coarse[...], window(ky, kx)) for kx in (2 * pair, 2 * pair + 1)]
            slabs = (a[:, :128], jnp.concatenate([a[:, 128:], b[:, :64]], 1), b[:, 64:])
            for n, slab in enumerate(slabs):
                p = 3 * pair + n
                part[ky, p] = slab.astype(BF16)
                if ky is xo:
                    along_x(xo, p, 1)
                elif ky is (xa, xb)[p % 2]:
                    along_x(ky, p, 0)

    total = None
    for t in range(16):
        term = nn(window(t // 4, t % 4), own_up[t])
        total = term if total is None else total + term
    c_pos[...] = total

    for k in range(nz):
        zz = lax.rem(z + 1 + k, nz)
        q = second(zz)
        for which in range(2):
            arrived(rx1.at[zz, which], x1r.at[zz, which])
        kept[k] = part[x, zz].astype(F32) + rx1[zz, 0].astype(F32)
        sb1[k] = (part[q, zz].astype(F32) + rx1[zz, 1].astype(F32)).astype(BF16)
        send(sb1.at[k], rx2.at[k], x2s.at[k], x2r.at[k], dev(q, z, y))

    def refine(n):
        acc = None
        for t in range(9):
            term = nn(hid[t // 3, pl.ds(16 * n + t % 3, 16)].reshape(256, COUT), mine[t])
            acc = term if acc is None else acc + term
        r_pos[pl.ds(256 * n, 256), :] = acc + conv_b[...]

    for n in range(4):
        refine(n)

    acc = None
    for k in range(nz):
        arrived(rx2.at[k], x2r.at[k])
        acc = kept[k] + rx2[k].astype(F32)
        if k < nz - 1:
            sb2[k] = acc.astype(BF16)
            send(sb2.at[k], rz.at[k], zs_s.at[k], zs_r.at[k], zpeers[k])
    for n in range(4, 8):
        refine(n)
    for k in range(nz - 1):
        arrived(rz.at[k], zs_r.at[k])
        acc = acc + rz[k].astype(F32)
    if ny == 2:
        ys[...] = acc
        send(ys, yr, y_sem.at[0], y_sem.at[1], ypeers[0])
    for r in range(2):
        for i in range(H):
            refined[2 * i + r] = r_pos[pl.ds(8 * r + i, 128, stride=16), :].T.astype(BF16)
    for i in range(H):
        c_grad[i] = c_pos[pl.ds(i, WC, stride=H), :].astype(BF16)
    if ny == 2:
        arrived(yr, y_sem.at[1])
        acc = acc + yr[...]
    res[x, z] = acc.astype(BF16)
    here = res.at[x, z]
    order = [d for k in range(1, nz // 2 + 1) for d in sorted({k, nz - k})]
    for d in order:
        send(here, here, azs.at[d - 1], azr.at[d - 1], zpeers[d - 1])
    for d in [0] + order:
        zz = lax.rem(z + nz - d, nz)
        got = res.at[x, zz]
        if d > 0:
            arrived(got, azr.at[d - 1])
        send(got, got, axs.at[0, zz], axr.at[0, zz], dev(second(zz), z, y))
        send(got, got, axs.at[1, zz], axr.at[1, zz], dev(first(zz), z, y))
    for d in [0] + order:
        zz = lax.rem(z + nz - d, nz)
        got = res.at[second(zz), zz]
        arrived(got, axr.at[0, zz])
        send(got, got, axs.at[2, zz], axr.at[2, zz], dev(first(zz), z, y))
    for d in [0] + order:
        zz = lax.rem(z + nz - d, nz)
        arrived(res.at[first(zz), zz], axr.at[1, zz])
        arrived(res.at[xo, zz], axr.at[2, zz])
    for copy in started:
        copy.wait_send()


def strip(dims, *args):
    nx, nz, ny = dims
    dma = pltpu.SemaphoreType.DMA
    vm = pltpu.VMEM
    any_ = pl.BlockSpec(memory_space=pl.ANY)
    return pl.pallas_call(
        functools.partial(kernel, dims),
        out_shape=(
            jax.ShapeDtypeStruct((2 * H, OWN_OUT, 2 * WC), BF16),
            jax.ShapeDtypeStruct((H, WC, OWN_IN), BF16),
            jax.ShapeDtypeStruct((nx, nz, PIECE, 128), BF16),
        ),
        in_specs=[VM, VM, VM, any_, any_, VM, VM],
        out_specs=[VM] * 3,
        scratch_shapes=[
            vm((CIN, POS), BF16),
            vm((COUT, FINE), BF16),
            vm((2, COUT, 128), BF16),
            vm((4, 4, COUT, CIN), BF16),
            vm((3, 3, COUT, COUT), BF16),
            vm((9, COUT, COUT), BF16),
            vm((9, COUT, OWN_OUT), BF16),
            vm((16, COUT, OWN_IN), BF16),
            vm((68, H, CIN), F32),
            vm((528, 6 * CIN), BF16),
            vm((66, 2, 2, H, COUT), F32),
            vm((66, 2, 2, H, COUT), F32),
            vm((3, 132, 16, COUT), BF16),
            vm((3, 132, 16, COUT), BF16),
            vm((2, 4, 66, H, COUT), F32),
            vm((nx, nz, PIECE, 128), BF16),
            vm((FINE, OWN_OUT), F32),
            vm((POS, OWN_IN), F32),
            vm((nz, 2, PIECE, 128), BF16),
            vm((nz, PIECE, 128), F32),
            vm((nz, PIECE, 128), BF16),
            vm((nz, PIECE, 128), BF16),
            vm((nz - 1, PIECE, 128), BF16),
            vm((nz - 1, PIECE, 128), BF16),
            vm((PIECE, 128), F32),
            vm((PIECE, 128), F32),
            dma((2,)), dma((3,)), dma((3,)), dma((3, PIECES)), dma((3, PIECES)), dma((2, 4)), dma((2, 4)),
            dma((nz, 2)), dma((nz, 2)), dma((nz,)), dma((nz,)), dma((nz - 1,)), dma((nz - 1,)), dma((2,)),
            dma((nz - 1,)), dma((nz - 1,)), dma((3, nz)), dma((3, nz)),
        ],
        compiler_params=pltpu.CompilerParams(
            collective_id=0, has_side_effects=True, vmem_limit_bytes=LIMIT
        ),
        name="strip",
    )(*args)


def unpack_kernel(src, up_grad, conv_grad):
    for ky in range(4):
        for pair in range(2):
            a, m, b = [src[ky, 3 * pair + n].astype(F32) for n in range(3)]
            up_grad[ky, 2 * pair] = jnp.concatenate([a, m[:, :64]], 1)
            up_grad[ky, 2 * pair + 1] = jnp.concatenate([m[:, 64:], b], 1)

    def block(b):
        return src[b // 4, 6 + b % 4 // 2, pl.ds(b % 2 * OWN_OUT, OWN_OUT), :].astype(F32)

    for t in range(9):
        tail = block(9 + t // 2)[:, 64 * (t % 2):64 * (t % 2) + 64]
        conv_grad[t // 3, t % 3] = jnp.concatenate([block(t), tail], 1)


def unpack(sums):
    return pl.pallas_call(
        unpack_kernel,
        out_shape=(
            jax.ShapeDtypeStruct((4, 4, OWN_IN, COUT), F32),
            jax.ShapeDtypeStruct((3, 3, OWN_OUT, COUT), F32),
        ),
        in_specs=[VM],
        out_specs=[VM] * 2,
        compiler_params=pltpu.CompilerParams(vmem_limit_bytes=LIMIT),
        name="unpack",
    )(sums)


def local(dims, coarse, up_weight, up_bias, conv_weight, conv_bias, cotangent):
    rank = lax.axis_index("chan")
    conv_b = lax.dynamic_slice_in_dim(conv_bias, rank * OWN_OUT, OWN_OUT).reshape(1, OWN_OUT)
    c = coarse.transpose(0, 2, 1).reshape(OWN_IN, POS)
    g = cotangent.reshape(OWN_OUT, H, 2, 2 * WC).transpose(0, 3, 2, 1).reshape(OWN_OUT, FINE)
    edge = jnp.concatenate(
        [g[:, :32], c[:48, :16], c[48:, :16], g[:, -32:], c[:48, -16:], c[48:, -16:]], 1
    )
    refined, c_grad, sums = strip(
        dims, c, g, edge, up_weight.transpose(0, 1, 3, 2), conv_weight, up_bias.reshape(1, COUT), conv_b
    )
    up_grad, conv_grad = unpack(sums)
    return refined.transpose(1, 0, 2), c_grad.transpose(2, 0, 1), up_grad, conv_grad.transpose(0, 1, 3, 2)


def solution(mesh):
    dims = {64: (4, 8, 2), 8: (4, 2, 1)}[mesh.shape["lon"]]
    placed = (P("chan", None, "lon"), P(), P(), P(), P(), P("chan", None, "lon"))
    return jax.shard_map(
        functools.partial(local, dims),
        mesh=mesh,
        in_specs=placed,
        out_specs=(
            P("chan", None, "lon"),
            P("chan", None, "lon"),
            P(None, None, "chan", None),
            P(None, None, None, "chan"),
        ),
        check_vma=False,
    )
```

time: 92 us -> 73.4 us (0.80); the launches traced: 90.7 us -> 73.1 us
  Pallas kernels: 75.7 us -> 64.3 us
  local copies, waits for them, and re-layouts: 14.3 us -> 8.12 us
    pallas_call x3 -> x1, Pallas kernels: 72.8 us -> 61.7 us  [strip(): pl.pallas_call(functools.partial(kernel, dims), out_shape=(jax.ShapeDtype...]
    unnamed x12 -> x8, local copies, waits for them, and re-layouts: 7.19 us -> 3.91 us
    pallas_call x2 -> x0, local copies, waits for them, and re-layouts: 2.22 us -> none  [compute(): pl.pallas_call(compute_kernel, out_shape=(jax.ShapeDtypeStruct((OWN_OUT,...]
where the time goes in v2:
time: 73.4 us; the launch traced here: 73.1 us
  Pallas kernels  64.3 us (88%)
  local copies, waits for them, and re-layouts  8.12 us (11%)
    pallas_call x1, Pallas kernels, strip(): pl.pallas_call(functools.partial(kernel, dims), out_shape=(jax.ShapeDtype...  61.7 us
    unnamed x8, local copies, waits for them, and re-layouts  3.91 us
    pallas_call x1, Pallas kernels, unpack(): pl.pallas_call(unpack_kernel, out_shape=(jax.ShapeDtypeStruct((4, 4, OWN_...  2.6 us
    reshape x2, local copies, waits for them, and re-layouts, local(): cotangent.reshape(OWN_OUT, H, 2, 2 * WC).transpose(0, 3, 2, 1)  1.67 us

profile of v2, /device:TPU:2, one launch (start us, length us, event | category | flops | bytes accessed | tf_op | source)
XLA Modules:
  0.0 73.1 jit_solution(3483330329826091222)
XLA Ops:
  0.6 0.0 copy-start
  0.6 0.7 copy-done
  1.3 0.6 dynamic-slice_bitcast_fusion.conv_b
  1.9 1.0 %copy.25 = bf16[96,64,8]{0,2,1:T(8,128)(2,1)S(1)} copy(bf16[96,64,8]{0,1,2:T(8,128)(2,1)} %bitcast.20) | data formatting | bytes 196608 | tf_op jit(solution)/shard_map/transpose | solution.py:428
  2.9 0.1 copy.21.coarse
  3.0 0.0 copy-start.2
  3.0 0.1 fusion.1
  3.1 1.5 %copy.14 = bf16[48,8,2,128]{0,1,2,3:T(8,128)(2,1)S(1)} copy(bf16[48,8,2,128]{3,2,1,0:T(2,128)(2,1)} %bitcast.19) | data formatting | bytes 393216 | tf_op jit(solution)/shard_map/reshape | solution.py:429
  4.6 0.2 copy.22.cot
  4.8 0.0 copy-start.1
  4.8 0.1 fusion
  4.9 0.7 concatenate.3.edge
  5.6 0.0 copy-done.2
  5.6 0.0 copy-done.1
  5.6 61.7 %strip.1 = (bf16[16,48,128]{2,1,0:T(8,128)(2,1)}, bf16[8,64,96]{2,1,0:T(8,128)(2,1)}, bf16[4,8,96,128]{3,2,1,0:T(8,128)(2,1)}) custom-call(bf16[96,512]{1,0:T(8,128)(2,1)} %copy-done.2, bf16[48,2048]{1,0:T(8,128)(2,1)} %copy-done.1, bf16[48,128]{1,0:T(8,128)(2,1)} %concatenate.3.edge, bf16[4,4,192,384]{3,2,1,0:T(8,128)(2,1)} %bitcast.15, ...), custom_call_target="tpu_custom_call" | custom-call | tf_op jit(solution)/shard_map/strip/pallas_call | solution.py:349
  67.3 1.7 %copy.23 = bf16[48,16,128]{2,1,0:T(8,128)(2,1)} copy(bf16[48,16,128]{2,0,1:T(8,128)(2,1)} %bitcast.18) | data formatting | bytes 393216
  69.0 2.6 %unpack.1 = (f32[4,4,96,192]{3,2,1,0:T(8,128)}, f32[3,3,48,192]{3,2,1,0:T(8,128)}) custom-call(bf16[4,8,96,128]{3,2,1,0:T(8,128)(2,1)} %get-tuple-element.11.src), custom_call_target="tpu_custom_call" | custom-call | tf_op jit(solution)/shard_map/unpack/pallas_call | solution.py:412
  71.6 1.6 %copy.27 = bf16[96,8,64]{0,2,1:T(8,128)(2,1)} copy(bf16[96,8,64]{0,2,1:T(8,128)(2,1)} %bitcast.21) | data formatting | bytes 196608
Async XLA Ops:
  0.6 0.7 copy-start
  3.0 2.6 %copy-start.2 = (bf16[96,512]{1,0:T(8,128)(2,1)}, bf16[96,512]{1,0:T(8,128)(2,1)S(1)}, u32[]{:S(2)}) copy-start(bf16[96,512]{1,0:T(8,128)(2,1)S(1)} %copy.21.coarse) | copy-start | bytes 294916
  4.8 0.8 %copy-start.1 = (bf16[48,2048]{1,0:T(8,128)(2,1)}, bf16[48,2048]{1,0:T(8,128)(2,1)S(1)}, u32[]{:S(2)}) copy-start(bf16[48,2048]{1,0:T(8,128)(2,1)S(1)} %copy.22.cot) | copy-start | bytes 589828

commit v3 on v2

--- a/solution.py
+++ b/solution.py
@@ -44,12 +44,12 @@
     return [jnp.concatenate(pair, 1).astype(BF16) for pair in pairs]
 
 
-def kernel(dims, coarse, cot, edge, up_hbm, conv_hbm, up_b, conv_b,
+def kernel(dims, coarse_hbm, cot_hbm, up_hbm, conv_hbm, up_b, conv_b,
            refined, c_grad, res,
-           c_all, g_all, e_all, up_w, conv_w, conv_t, mine, own_up,
+           coarse_in, cot_in, coarse, cot, edge, g32, c_all, g_all, e_all, up_w, conv_w, conv_t, mine, own_up,
            xf, xl, pre, fs, hid, cots, df, part, r_pos, c_pos,
-           rx1, kept, sb1, rx2, sb2, rz, ys, yr,
-           w_sem, cs, cr, gs, gr, es, er, x1s, x1r, x2s, x2r, zs_s, zs_r, y_sem,
+           rx1, kept, sb1, rx2, sb2, rz,
+           w_sem, cs, cr, gs, gr, es, er, x1s, x1r, x2s, x2r, zs_s, zs_r,
            azs, azr, axs, axr):
     nx, nz, ny = dims
     lon, rank = lax.axis_index("lon"), lax.axis_index("chan")
@@ -71,12 +71,19 @@
     def second(zz):
         return xb + lax.rem(zz, 2) * (xa - xb)
 
-    zpeers = [dev(x, lax.rem(z + d, nz), y) for d in range(1, nz)]
-    ypeers = [dev(x, z, 1 - y)] if ny == 2 else []
+    links = sorted(
+        [(d, f) for d in range(nz) for f in range(ny)], key=lambda v: min(v[0], nz - v[0]) + 2 * v[1]
+    )
+    zy = {(d, f): dev(x, lax.rem(z + d, nz), lax.rem(y + f, ny)) for d, f in links}
+
+    def slot(d, f):
+        return ny * d + f
 
     loads = [
-        pltpu.make_async_copy(up_hbm, up_w, w_sem.at[0]),
-        pltpu.make_async_copy(conv_hbm, conv_w, w_sem.at[1]),
+        pltpu.make_async_copy(coarse_hbm, coarse_in, w_sem.at[0]),
+        pltpu.make_async_copy(cot_hbm, cot_in, w_sem.at[1]),
+        pltpu.make_async_copy(up_hbm, up_w, w_sem.at[2]),
+        pltpu.make_async_copy(conv_hbm, conv_w, w_sem.at[3]),
     ]
     for load in loads:
         load.start()
@@ -84,9 +91,31 @@
     barrier = pltpu.get_barrier_semaphore()
     greet = [(lon, lax.rem(rank + d, 4)) for d in range(1, 4)]
     greet += [(side, lax.rem(rank + d, 4)) for side in sides for d in range(4)]
-    greet += [dev(xa, z, y), dev(xb, z, y)] + zpeers + ypeers
+    greet += [dev(xa, z, y), dev(xb, z, y), dev(xo, z, y)] + [zy[v] for v in links[1:]]
     for peer in greet:
         pl.semaphore_signal(barrier, inc=1, device_id=peer, device_id_type=MESH)
+
+    loads[0].wait()
+    for i in range(H):
+        c_pos[pl.ds(i, WC, stride=H), :] = coarse_in[i].astype(F32)
+    for n in range(4):
+        coarse[:, pl.ds(128 * n, 128)] = c_pos[pl.ds(128 * n, 128), :].T.astype(BF16)
+    loads[1].wait()
+    g32[...] = cot_in[...].astype(F32).reshape(OWN_OUT * 16, 128)
+    for r in range(2):
+        for i in range(H):
+            r_pos[pl.ds(8 * r + i, 128, stride=16), :] = g32[pl.ds(2 * i + r, OWN_OUT, stride=16), :].T
+    for n in range(16):
+        cot[:, pl.ds(128 * n, 128)] = r_pos[pl.ds(128 * n, 128), :].T.astype(BF16)
+    ends = []
+    for c0, g0 in ((0, 0), (POS - 16, FINE - 32)):
+        c_end = coarse[:, pl.ds(c0, 16)].astype(F32)
+        ends += [cot[:, pl.ds(g0, 32)].astype(F32), c_end[:OWN_OUT], c_end[OWN_OUT:]]
+    edge[...] = jnp.concatenate(ends, 1).astype(BF16)
+    pad = jnp.zeros((132, 16, 64), BF16)
+    for m in range(3):
+        cots[:, :, pl.ds(256 * m + COUT, 64)] = pad
+    conv_t[...] = jnp.zeros(conv_t.shape, BF16)
     pl.semaphore_wait(barrier, len(greet))
 
     started = []
@@ -131,15 +160,18 @@
         arrived(g_block(cross, k), gr.at[0, k])
         send(g_block(cross, k), g_block(cross, k), gs.at[2, k], gr.at[2, k], (lon, sib))
 
-    for load in loads:
+    for load in loads[2:]:
         load.wait()
+    own_bias = jnp.zeros((1, OWN_OUT), F32)
+    for r in range(4):
+        own_bias += jnp.where(rank == r, conv_b[:, pl.ds(OWN_OUT * r, OWN_OUT)], 0.0)
     a_of = lax.broadcasted_iota(jnp.int32, (COUT, OWN_OUT), 0)
     b_of = lax.broadcasted_iota(jnp.int32, (COUT, OWN_OUT), 1)
     pick = (a_of == b_of + OWN_OUT * rank).astype(F32).astype(BF16)
     for t in range(9):
         w = conv_w[t // 3, t % 3]
         mine[t] = nn(w, pick).astype(BF16)
-        conv_t[t] = w.astype(F32).T.astype(BF16)
+        conv_t[pl.ds(768 * (t % 3) + 256 * (2 - t // 3), COUT), :] = w.astype(F32).T.astype(BF16)
     src = lax.broadcasted_iota(jnp.int32, (COUT, CIN), 0)
     dst = lax.broadcasted_iota(jnp.int32, (COUT, CIN), 1)
     place = src // OWN_OUT * OWN_IN + lax.rem(src, OWN_OUT)
@@ -231,7 +263,7 @@
 
     def place_cot(at, v, n):
         for m, w in enumerate(shifted(v.reshape(n, 2, H, COUT))):
-            cots[m, pl.ds(at, n)] = w
+            cots[pl.ds(at, n), :, pl.ds(256 * m, COUT)] = w
 
     place_cot(0, left[64:96], 2)
     place_cot(130, right[0:32], 2)
@@ -240,12 +272,8 @@
 
     @pl.loop(0, 5)
     def _(n):
-        acc = None
-        for ky in range(3):
-            for kx in range(3):
-                g = cots[2 - ky, pl.ds(n * 26 + 2 - kx, 26)].reshape(416, COUT)
-                term = nn(g, conv_t[ky * 3 + kx])
-                acc = term if acc is None else acc + term
+        g = [cots[pl.ds(n * 26 + 2 - kx, 26)].reshape(416, 768) for kx in range(3)]
+        acc = nn(jnp.concatenate(g, 1), conv_t[...])
         ts = pl.ds(n * 13, 13)
         d = (acc.reshape(13, 2, 2, H, COUT) * fs[ts]).astype(BF16).astype(F32)
         for cp in range(2):
@@ -274,69 +302,95 @@
         total = term if total is None else total + term
     c_pos[...] = total
 
-    for k in range(nz):
-        zz = lax.rem(z + 1 + k, nz)
+    far_first = sorted(range(nz), key=lambda d: -min(d, nz - d))
+    for d in far_first:
+        zz = lax.rem(z + d, nz)
         q = second(zz)
         for which in range(2):
             arrived(rx1.at[zz, which], x1r.at[zz, which])
-        kept[k] = part[x, zz].astype(F32) + rx1[zz, 0].astype(F32)
-        sb1[k] = (part[q, zz].astype(F32) + rx1[zz, 1].astype(F32)).astype(BF16)
-        send(sb1.at[k], rx2.at[k], x2s.at[k], x2r.at[k], dev(q, z, y))
+        kept[d] = part[x, zz].astype(F32) + rx1[zz, 0].astype(F32)
+        sb1[d] = (part[q, zz].astype(F32) + rx1[zz, 1].astype(F32)).astype(BF16)
+        send(sb1.at[d], rx2.at[d], x2s.at[d], x2r.at[d], dev(q, z, y))
 
     def refine(n):
         acc = None
         for t in range(9):
             term = nn(hid[t // 3, pl.ds(16 * n + t % 3, 16)].reshape(256, COUT), mine[t])
             acc = term if acc is None else acc + term
-        r_pos[pl.ds(256 * n, 256), :] = acc + conv_b[...]
+        r_pos[pl.ds(256 * n, 256), :] = acc + own_bias
 
     for n in range(4):
         refine(n)
 
-    acc = None
-    for k in range(nz):
-        arrived(rx2.at[k], x2r.at[k])
-        acc = kept[k] + rx2[k].astype(F32)
-        if k < nz - 1:
-            sb2[k] = acc.astype(BF16)
-            send(sb2.at[k], rz.at[k], zs_s.at[k], zs_r.at[k], zpeers[k])
+    half = PIECE // ny
+
+    def part_of(h):
+        return pl.ds(pl.multiple_of(h * half, 16), half)
+
+    for d in far_first:
+        arrived(rx2.at[d], x2r.at[d])
+        total = kept[d] + rx2[d].astype(F32)
+        kept[d] = total
+        sb2[d] = total.astype(BF16)
+        for f in range(ny - 1, -1, -1):
+            if (d, f) != (0, 0):
+                h = part_of(lax.rem(y + f, ny))
+                send(sb2.at[d, h, :], rz.at[slot(d, f)], zs_s.at[slot(d, f)], zs_r.at[slot(d, f)], zy[d, f])
     for n in range(4, 8):
         refine(n)
-    for k in range(nz - 1):
-        arrived(rz.at[k], zs_r.at[k])
-        acc = acc + rz[k].astype(F32)
-    if ny == 2:
-        ys[...] = acc
-        send(ys, yr, y_sem.at[0], y_sem.at[1], ypeers[0])
+    for i in range(H):
+        c_grad[i] = c_pos[pl.ds(i, WC, stride=H), :].astype(BF16)
+    mine_rows = part_of(y)
+    acc = kept[0, mine_rows, :]
+    for d, f in links[1:]:
+        arrived(rz.at[slot(d, f)], zs_r.at[slot(d, f)])
+        acc = acc + rz[slot(d, f)].astype(F32)
+    res[x, z, mine_rows, :] = acc.astype(BF16)
+    here = res.at[x, z, mine_rows, :]
+    for d, f in links[:0:-1]:
+        send(here, here, azs.at[slot(d, f)], azr.at[slot(d, f)], zy[d, f])
+
     for r in range(2):
         for i in range(H):
-            refined[2 * i + r] = r_pos[pl.ds(8 * r + i, 128, stride=16), :].T.astype(BF16)
-    for i in range(H):
-        c_grad[i] = c_pos[pl.ds(i, WC, stride=H), :].astype(BF16)
-    if ny == 2:
-        arrived(yr, y_sem.at[1])
-        acc = acc + yr[...]
-    res[x, z] = acc.astype(BF16)
-    here = res.at[x, z]
-    order = [d for k in range(1, nz // 2 + 1) for d in sorted({k, nz - k})]
-    for d in order:
-        send(here, here, azs.at[d - 1], azr.at[d - 1], zpeers[d - 1])
-    for d in [0] + order:
-        zz = lax.rem(z + nz - d, nz)
-        got = res.at[x, zz]
-        if d > 0:
-            arrived(got, azr.at[d - 1])
-        send(got, got, axs.at[0, zz], axr.at[0, zz], dev(second(zz), z, y))
-        send(got, got, axs.at[1, zz], axr.at[1, zz], dev(first(zz), z, y))
-    for d in [0] + order:
-        zz = lax.rem(z + nz - d, nz)
-        got = res.at[second(zz), zz]
-        arrived(got, axr.at[0, zz])
-        send(got, got, axs.at[2, zz], axr.at[2, zz], dev(first(zz), z, y))
-    for d in [0] + order:
-        zz = lax.rem(z + nz - d, nz)
-        arrived(res.at[first(zz), zz], axr.at[1, zz])
-        arrived(res.at[xo, zz], axr.at[2, zz])
+            g32[pl.ds(2 * i + r, OWN_OUT, stride=16), :] = r_pos[pl.ds(8 * r + i, 128, stride=16), :].T
+    refined[...] = g32[...].reshape(OWN_OUT, 16, 128).astype(BF16)
+
+    def origin(d, f):
+        return lax.rem(z + nz - d, nz), part_of(lax.rem(y + f, ny))
+
+    def direct(d):
+        return d == nz // 2
+
+    def spread_x(d, f):
+        zz, rows = origin(d, f)
+        n = slot(d, f)
+        got = res.at[x, zz, rows, :]
+        if (d, f) != (0, 0):
+            arrived(got, azr.at[n])
+        if direct(d):
+            send(got, got, axs.at[2, n], axr.at[2, n], dev(xo, z, y))
+        send(got, got, axs.at[0, n], axr.at[0, n], dev(second(zz), z, y))
+        send(got, got, axs.at[1, n], axr.at[1, n], dev(first(zz), z, y))
+
+    def forward_x(d, f):
+        zz, rows = origin(d, f)
+        n = slot(d, f)
+        got = res.at[second(zz), zz, rows, :]
+        arrived(got, axr.at[0, n])
+        if not direct(d):
+            send(got, got, axs.at[2, n], axr.at[2, n], dev(first(zz), z, y))
+
+    lag = 4
+    for n in range(len(links) + lag):
+        if n < len(links):
+            spread_x(*links[n])
+        if n >= lag:
+            forward_x(*links[n - lag])
+    for d, f in links:
+        zz, rows = origin(d, f)
+        n = slot(d, f)
+        arrived(res.at[first(zz), zz, rows, :], axr.at[1, n])
+        arrived(res.at[xo, zz, rows, :], axr.at[2, n])
     for copy in started:
         copy.wait_send()
 
@@ -349,19 +403,25 @@
     return pl.pallas_call(
         functools.partial(kernel, dims),
         out_shape=(
-            jax.ShapeDtypeStruct((2 * H, OWN_OUT, 2 * WC), BF16),
+            jax.ShapeDtypeStruct((OWN_OUT, 2 * H, 2 * WC), BF16),
             jax.ShapeDtypeStruct((H, WC, OWN_IN), BF16),
             jax.ShapeDtypeStruct((nx, nz, PIECE, 128), BF16),
         ),
-        in_specs=[VM, VM, VM, any_, any_, VM, VM],
+        in_specs=[any_] * 4 + [VM] * 2,
         out_specs=[VM] * 3,
         scratch_shapes=[
+            vm((H, WC, OWN_IN), BF16),
+            vm((OWN_OUT, 2 * H, 2 * WC), BF16),
+            vm((OWN_IN, POS), BF16),
+            vm((OWN_OUT, FINE), BF16),
+            vm((OWN_OUT, 128), BF16),
+            vm((OWN_OUT * 2 * H, 2 * WC), F32),
             vm((CIN, POS), BF16),
             vm((COUT, FINE), BF16),
             vm((2, COUT, 128), BF16),
             vm((4, 4, COUT, CIN), BF16),
             vm((3, 3, COUT, COUT), BF16),
-            vm((9, COUT, COUT), BF16),
+            vm((9 * 256, COUT), BF16),
             vm((9, COUT, OWN_OUT), BF16),
             vm((16, COUT, OWN_IN), BF16),
             vm((68, H, CIN), F32),
@@ -369,7 +429,7 @@
             vm((66, 2, 2, H, COUT), F32),
             vm((66, 2, 2, H, COUT), F32),
             vm((3, 132, 16, COUT), BF16),
-            vm((3, 132, 16, COUT), BF16),
+            vm((132, 16, 3 * 256), BF16),
             vm((2, 4, 66, H, COUT), F32),
             vm((nx, nz, PIECE, 128), BF16),
             vm((FINE, OWN_OUT), F32),
@@ -378,13 +438,11 @@
             vm((nz, PIECE, 128), F32),
             vm((nz, PIECE, 128), BF16),
             vm((nz, PIECE, 128), BF16),
-            vm((nz - 1, PIECE, 128), BF16),
-            vm((nz - 1, PIECE, 128), BF16),
-            vm((PIECE, 128), F32),
-            vm((PIECE, 128), F32),
-            dma((2,)), dma((3,)), dma((3,)), dma((3, PIECES)), dma((3, PIECES)), dma((2, 4)), dma((2, 4)),
-            dma((nz, 2)), dma((nz, 2)), dma((nz,)), dma((nz,)), dma((nz - 1,)), dma((nz - 1,)), dma((2,)),
-            dma((nz - 1,)), dma((nz - 1,)), dma((3, nz)), dma((3, nz)),
+            vm((nz, PIECE, 128), BF16),
+            vm((nz * ny, PIECE // ny, 128), BF16),
+            dma((4,)), dma((3,)), dma((3,)), dma((3, PIECES)), dma((3, PIECES)), dma((2, 4)), dma((2, 4)),
+            dma((nz, 2)), dma((nz, 2)), dma((nz,)), dma((nz,)), dma((nz * ny,)), dma((nz * ny,)),
+            dma((nz * ny,)), dma((nz * ny,)), dma((3, nz * ny)), dma((3, nz * ny)),
         ],
         compiler_params=pltpu.CompilerParams(
             collective_id=0, has_side_effects=True, vmem_limit_bytes=LIMIT
@@ -393,52 +451,74 @@
     )(*args)
 
 
-def unpack_kernel(src, up_grad, conv_grad):
+def unpack_kernel(refined, c_grad, sums, refined_out, c_out, up_grad, conv_grad, src, up, conv, sems, out_sems):
+    nx = sums.shape[0]
+    passes = [
+        pltpu.make_async_copy(refined, refined_out, out_sems.at[nx]),
+        pltpu.make_async_copy(c_grad, c_out, out_sems.at[nx + 1]),
+    ]
+    loads = [pltpu.make_async_copy(sums.at[k], src.at[k], sems.at[k]) for k in range(nx)]
+    for copy in loads + passes:
+        copy.start()
     for ky in range(4):
+        loads[ky].wait()
         for pair in range(2):
             a, m, b = [src[ky, 3 * pair + n].astype(F32) for n in range(3)]
-            up_grad[ky, 2 * pair] = jnp.concatenate([a, m[:, :64]], 1)
-            up_grad[ky, 2 * pair + 1] = jnp.concatenate([m[:, 64:], b], 1)
+            up[ky, 2 * pair] = jnp.concatenate([a, m[:, :64]], 1)
+            up[ky, 2 * pair + 1] = jnp.concatenate([m[:, 64:], b], 1)
+        copy = pltpu.make_async_copy(up.at[ky], up_grad.at[ky], out_sems.at[ky])
+        copy.start()
+        passes.append(copy)
 
     def block(b):
         return src[b // 4, 6 + b % 4 // 2, pl.ds(b % 2 * OWN_OUT, OWN_OUT), :].astype(F32)
 
     for t in range(9):
         tail = block(9 + t // 2)[:, 64 * (t % 2):64 * (t % 2) + 64]
-        conv_grad[t // 3, t % 3] = jnp.concatenate([block(t), tail], 1)
-
-
-def unpack(sums):
+        conv[t // 3, t % 3] = jnp.concatenate([block(t), tail], 1)
+    copy = pltpu.make_async_copy(conv, conv_grad, out_sems.at[nx + 2])
+    copy.start()
+    for copy in passes + [copy]:
+        copy.wait()
+
+
+def unpack(refined, c_grad, sums):
+    any_ = pl.BlockSpec(memory_space=pl.ANY)
+    up = (4, 4, OWN_IN, COUT)
+    conv = (3, 3, OWN_OUT, COUT)
     return pl.pallas_call(
         unpack_kernel,
         out_shape=(
-            jax.ShapeDtypeStruct((4, 4, OWN_IN, COUT), F32),
-            jax.ShapeDtypeStruct((3, 3, OWN_OUT, COUT), F32),
+            jax.ShapeDtypeStruct(refined.shape, BF16),
+            jax.ShapeDtypeStruct(c_grad.shape, BF16),
+            jax.ShapeDtypeStruct(up, F32),
+            jax.ShapeDtypeStruct(conv, F32),
         ),
-        in_specs=[VM],
-        out_specs=[VM] * 2,
+        in_specs=[any_] * 3,
+        out_specs=[any_] * 4,
+        scratch_shapes=[
+            pltpu.VMEM(sums.shape, BF16),
+            pltpu.VMEM(up, F32),
+            pltpu.VMEM(conv, F32),
+            pltpu.SemaphoreType.DMA((4,)),
+            pltpu.SemaphoreType.DMA((7,)),
+        ],
         compiler_params=pltpu.CompilerParams(vmem_limit_bytes=LIMIT),
         name="unpack",
-    )(sums)
+    )(refined, c_grad, sums)
 
 
 def local(dims, coarse, up_weight, up_bias, conv_weight, conv_bias, cotangent):
-    rank = lax.axis_index("chan")
-    conv_b = lax.dynamic_slice_in_dim(conv_bias, rank * OWN_OUT, OWN_OUT).reshape(1, OWN_OUT)
-    c = coarse.transpose(0, 2, 1).reshape(OWN_IN, POS)
-    g = cotangent.reshape(OWN_OUT, H, 2, 2 * WC).transpose(0, 3, 2, 1).reshape(OWN_OUT, FINE)
-    edge = jnp.concatenate(
-        [g[:, :32], c[:48, :16], c[48:, :16], g[:, -32:], c[:48, -16:], c[48:, -16:]], 1
+    refined, c_grad, sums = strip(
+        dims, coarse.transpose(1, 2, 0), cotangent, up_weight.transpose(0, 1, 3, 2), conv_weight,
+        up_bias.reshape(1, COUT), conv_bias.reshape(1, COUT),
     )
-    refined, c_grad, sums = strip(
-        dims, c, g, edge, up_weight.transpose(0, 1, 3, 2), conv_weight, up_bias.reshape(1, COUT), conv_b
-    )
-    up_grad, conv_grad = unpack(sums)
-    return refined.transpose(1, 0, 2), c_grad.transpose(2, 0, 1), up_grad, conv_grad.transpose(0, 1, 3, 2)
+    refined, c_grad, up_grad, conv_grad = unpack(refined, c_grad, sums)
+    return refined, c_grad.transpose(2, 0, 1), up_grad, conv_grad.transpose(0, 1, 3, 2)
 
 
 def solution(mesh):
-    dims = {64: (4, 8, 2), 8: (4, 2, 1)}[mesh.shape["lon"]]
+    dims = (4, 8, 2)
     placed = (P("chan", None, "lon"), P(), P(), P(), P(), P("chan", None, "lon"))
     return jax.shard_map(
         functools.partial(local, dims),

time: 73.4 us -> 76.9 us (1.048); the launches traced: 73.1 us -> 75.7 us
  Pallas kernels: 64.3 us -> 74.9 us
  local copies, waits for them, and re-layouts: 8.12 us -> 0 us
    pallas_call x1, Pallas kernels: 2.6 us -> 11.1 us  [unpack(): pl.pallas_call(unpack_kernel, out_shape=(jax.ShapeDtypeStruct(refined.sha...]
    unnamed x8 -> x0, local copies, waits for them, and re-layouts: 3.91 us -> none
    reshape x4 -> x0, local copies, waits for them, and re-layouts: 2.36 us -> none  [the longest x2 1.67 us: local(): cotangent.reshape(OWN_OUT, H, 2, 2 * WC).transpose(0, 3, 2, 1)]
    pallas_call x1, Pallas kernels: 61.7 us -> 63.8 us  [strip(): pl.pallas_call(functools.partial(kernel, dims), out_shape=(jax.ShapeDtype...]
    transpose x1 -> x0, local copies, waits for them, and re-layouts: 0.99 us -> none  [local(): c = coarse.transpose(0, 2, 1).reshape(OWN_IN, POS)]
where the time goes in v3:
time: 76.9 us; the launch traced here: 75.7 us
  Pallas kernels  74.9 us (97%)
  between operations  0.8 us (1%)
    pallas_call x1, Pallas kernels, strip(): pl.pallas_call(functools.partial(kernel, dims), out_shape=(jax.ShapeDtype...  63.8 us
    pallas_call x1, Pallas kernels, unpack(): pl.pallas_call(unpack_kernel, out_shape=(jax.ShapeDtypeStruct(refined.sha...  11.1 us

profile of v3, /device:TPU:2, one launch (start us, length us, event | category | flops | bytes accessed | tf_op | source)
XLA Modules:
  0.0 75.7 jit_solution(11534080747166356890)
XLA Ops:
  0.6 63.8 %strip.1 = (bf16[48,16,128]{2,1,0:T(8,128)(2,1)}, bf16[8,64,96]{2,1,0:T(8,128)(2,1)}, bf16[4,8,96,128]{3,2,1,0:T(8,128)(2,1)}) custom-call(bf16[8,64,96]{2,1,0:T(8,128)(2,1)} %bitcast.7, bf16[48,16,128]{2,1,0:T(8,128)(2,1)} %cot_hbm.1, bf16[4,4,192,384]{3,2,1,0:T(8,128)(2,1)} %bitcast.6, bf16[3,3,192,192]{3,2,1,0:T(8,128)(2,1)} %conv_hbm.1, ...), custom_call_target="tpu_custom_call" | custom-call | tf_op jit(solution)/shard_map/strip/pallas_call | solution.py:403
  64.4 11.1 %unpack.1 = (bf16[48,16,128]{2,1,0:T(8,128)(2,1)}, bf16[8,64,96]{2,1,0:T(8,128)(2,1)}, f32[4,4,96,192]{3,2,1,0:T(8,128)}, f32[3,3,48,192]{3,2,1,0:T(8,128)}) custom-call(bf16[48,16,128]{2,1,0:T(8,128)(2,1)} %get-tuple-element.11.refined, bf16[8,64,96]{2,1,0:T(8,128)(2,1)} %get-tuple-element.12.c_grad, bf16[4,8,96,128]{3,2,1,0:T(8,128)(2,1)} %get-tuple-element.13.sums), custom_call_target="tpu_custom_call" | custom-call | tf_op jit(solution)/shard_map/unpack/pallas_call | solution.py:489

commit v4 on v3

--- a/solution.py
+++ b/solution.py
@@ -48,8 +48,8 @@
            refined, c_grad, res,
            coarse_in, cot_in, coarse, cot, edge, g32, c_all, g_all, e_all, up_w, conv_w, conv_t, mine, own_up,
            xf, xl, pre, fs, hid, cots, df, part, r_pos, c_pos,
-           rx1, kept, sb1, rx2, sb2, rz,
-           w_sem, cs, cr, gs, gr, es, er, x1s, x1r, x2s, x2r, zs_s, zs_r,
+           rx1, kept, sb1, rx2, sb2, rz, ys, yr,
+           w_sem, cs, cr, gs, gr, es, er, x1s, x1r, x2s, x2r, zs_s, zs_r, y_sem,
            azs, azr, axs, axr):
     nx, nz, ny = dims
     lon, rank = lax.axis_index("lon"), lax.axis_index("chan")
@@ -71,13 +71,10 @@
     def second(zz):
         return xb + lax.rem(zz, 2) * (xa - xb)
 
-    links = sorted(
-        [(d, f) for d in range(nz) for f in range(ny)], key=lambda v: min(v[0], nz - v[0]) + 2 * v[1]
-    )
-    zy = {(d, f): dev(x, lax.rem(z + d, nz), lax.rem(y + f, ny)) for d, f in links}
-
-    def slot(d, f):
-        return ny * d + f
+    near_first = sorted(range(nz), key=lambda d: min(d, nz - d))
+    far_first = near_first[::-1]
+    zdev = [dev(x, lax.rem(z + d, nz), y) for d in range(nz)]
+    ydev = dev(x, z, 1 - y)
 
     loads = [
         pltpu.make_async_copy(coarse_hbm, coarse_in, w_sem.at[0]),
@@ -89,9 +86,10 @@
         load.start()
 
     barrier = pltpu.get_barrier_semaphore()
-    greet = [(lon, lax.rem(rank + d, 4)) for d in range(1, 4)]
+    greet = [zdev[d] for d in far_first[:-1]]
     greet += [(side, lax.rem(rank + d, 4)) for side in sides for d in range(4)]
-    greet += [dev(xa, z, y), dev(xb, z, y), dev(xo, z, y)] + [zy[v] for v in links[1:]]
+    greet += [dev(xo, z, y), dev(xa, z, y), dev(xb, z, y)]
+    greet += [(lon, lax.rem(rank + d, 4)) for d in range(1, 4)]
     for peer in greet:
         pl.semaphore_signal(barrier, inc=1, device_id=peer, device_id_type=MESH)
 
@@ -100,6 +98,36 @@
         c_pos[pl.ds(i, WC, stride=H), :] = coarse_in[i].astype(F32)
     for n in range(4):
         coarse[:, pl.ds(128 * n, 128)] = c_pos[pl.ds(128 * n, 128), :].T.astype(BF16)
+    pl.semaphore_wait(barrier, len(greet))
+
+    started = []
+
+    def copy_of(a, b, s, r, to):
+        return pltpu.make_async_remote_copy(
+            src_ref=a, dst_ref=b, send_sem=s, recv_sem=r, device_id=to, device_id_type=MESH
+        )
+
+    def send(a, b, s, r, to):
+        copy = copy_of(a, b, s, r, to)
+        copy.start()
+        started.append(copy)
+
+    def arrived(b, r):
+        copy_of(b, b, r, r, (lon, sib)).wait_recv()
+
+    def c_block(r):
+        return c_all.at[pl.ds(pl.multiple_of(r * OWN_IN, 16), OWN_IN), :]
+
+    width = FINE // PIECES
+
+    def g_block(r, k):
+        return g_all.at[pl.ds(pl.multiple_of(r * OWN_OUT, 16), OWN_OUT), pl.ds(k * width, width)]
+
+    def e_block(n, r):
+        return e_all.at[n, pl.ds(pl.multiple_of(r * OWN_OUT, 16), OWN_OUT), :]
+
+    send(coarse, c_block(rank), cs.at[0], cr.at[0], (lon, cross))
+    send(coarse, c_block(rank), cs.at[1], cr.at[1], (lon, sib))
     loads[1].wait()
     g32[...] = cot_in[...].astype(F32).reshape(OWN_OUT * 16, 128)
     for r in range(2):
@@ -112,40 +140,6 @@
         c_end = coarse[:, pl.ds(c0, 16)].astype(F32)
         ends += [cot[:, pl.ds(g0, 32)].astype(F32), c_end[:OWN_OUT], c_end[OWN_OUT:]]
     edge[...] = jnp.concatenate(ends, 1).astype(BF16)
-    pad = jnp.zeros((132, 16, 64), BF16)
-    for m in range(3):
-        cots[:, :, pl.ds(256 * m + COUT, 64)] = pad
-    conv_t[...] = jnp.zeros(conv_t.shape, BF16)
-    pl.semaphore_wait(barrier, len(greet))
-
-    started = []
-
-    def copy_of(a, b, s, r, to):
-        return pltpu.make_async_remote_copy(
-            src_ref=a, dst_ref=b, send_sem=s, recv_sem=r, device_id=to, device_id_type=MESH
-        )
-
-    def send(a, b, s, r, to):
-        copy = copy_of(a, b, s, r, to)
-        copy.start()
-        started.append(copy)
-
-    def arrived(b, r):
-        copy_of(b, b, r, r, (lon, sib)).wait_recv()
-
-    def c_block(r):
-        return c_all.at[pl.ds(pl.multiple_of(r * OWN_IN, 16), OWN_IN), :]
-
-    width = FINE // PIECES
-
-    def g_block(r, k):
-        return g_all.at[pl.ds(pl.multiple_of(r * OWN_OUT, 16), OWN_OUT), pl.ds(k * width, width)]
-
-    def e_block(n, r):
-        return e_all.at[n, pl.ds(pl.multiple_of(r * OWN_OUT, 16), OWN_OUT), :]
-
-    send(coarse, c_block(rank), cs.at[0], cr.at[0], (lon, cross))
-    send(coarse, c_block(rank), cs.at[1], cr.at[1], (lon, sib))
     for n, side in enumerate(sides):
         for d in range(4):
             send(edge, e_block(n, rank), es.at[n, d], er.at[n, d], (side, lax.rem(rank + d, 4)))
@@ -160,6 +154,10 @@
         arrived(g_block(cross, k), gr.at[0, k])
         send(g_block(cross, k), g_block(cross, k), gs.at[2, k], gr.at[2, k], (lon, sib))
 
+    pad = jnp.zeros((132, 16, 64), BF16)
+    for m in range(3):
+        cots[:, :, pl.ds(256 * m + COUT, 64)] = pad
+    conv_t[...] = jnp.zeros(conv_t.shape, BF16)
     for load in loads[2:]:
         load.wait()
     own_bias = jnp.zeros((1, OWN_OUT), F32)
@@ -216,7 +214,8 @@
             w = jnp.concatenate([up_w[ky, cp + 2 * d] for ky in taps for d in range(2)], 1)
             val = nt(xl[:, pl.ds(rp * 2 * CIN, 4 * CIN)], w)
             pre[:, cp, rp] = val.reshape(66, H, COUT)
-        pass_on(1 + rp)
+            if (rp, cp) != (1, 1):
+                pass_on(1 + 2 * rp + cp)
 
     bias = up_b[...].reshape(1, 1, 1, 1, COUT)
 
@@ -230,11 +229,46 @@
         for m, w in enumerate(shifted(h)):
             hid[m, pl.ds(n * 6, 6)] = w
 
-    pass_on(3)
-
     def along_x(chunk, p, which):
         send(part.at[chunk, p], rx1.at[p, which], x1s.at[p, which], x1r.at[p, which],
              dev(first(p), z, y))
+
+    def place_cot(at, v, n):
+        for m, w in enumerate(shifted(v.reshape(n, 2, H, COUT))):
+            cots[pl.ds(at, n), :, pl.ds(256 * m, COUT)] = w
+
+    place_cot(0, left[64:96], 2)
+    place_cot(130, right[0:32], 2)
+    cols = 2 * WC // PIECES
+    for k in range(PIECES):
+        arrived(g_block(sib, k), gr.at[1, k])
+        arrived(g_block(diag, k), gr.at[2, k])
+        for b in range(k * cols // 8, (k + 1) * cols // 8):
+            place_cot(2 + 8 * b, g_all[:, pl.ds(128 * b, 128)].astype(F32).T, 8)
+        count = cols + 2 * (k == PIECES - 1)
+        g = [cots[pl.ds(k * cols + 2 - kx, count)].reshape(16 * count, 768) for kx in range(3)]
+        acc = nn(jnp.concatenate(g, 1), conv_t[...])
+        ts = pl.ds(k * cols // 2, count // 2)
+        d = (acc.reshape(count // 2, 2, 2, H, COUT) * fs[ts]).astype(BF16).astype(F32)
+        for cp in range(2):
+            even, odd = d[:, cp, 0], d[:, cp, 1]
+            for ky, v in enumerate((down(odd), even, odd, up(even))):
+                df[cp, ky, ts] = v
+
+    def window(ky, kx):
+        return df[kx % 2, ky, pl.ds(kx // 2, 64)].reshape(POS, COUT).astype(BF16)
+
+    for ky in (xo, xa, xb, x):
+        for pair in range(2):
+            a, b = [nn(coarse[...], window(ky, kx)) for kx in (2 * pair, 2 * pair + 1)]
+            slabs = (a[:, :128], jnp.concatenate([a[:, 128:], b[:, :64]], 1), b[:, 64:])
+            for n, slab in enumerate(slabs):
+                p = 3 * pair + n
+                part[ky, p] = slab.astype(BF16)
+                if ky is xo:
+                    along_x(xo, p, 1)
+                elif ky is (xa, xb)[p % 2]:
+                    along_x(ky, p, 0)
 
     def spot(b):
         return b // 4, 6 + b % 4 // 2, pl.ds(b % 2 * OWN_OUT, OWN_OUT)
@@ -257,52 +291,12 @@
         along_x(xo, p, 1)
         along_x(first(p), p, 0)
 
-    for k in range(PIECES):
-        arrived(g_block(sib, k), gr.at[1, k])
-        arrived(g_block(diag, k), gr.at[2, k])
-
-    def place_cot(at, v, n):
-        for m, w in enumerate(shifted(v.reshape(n, 2, H, COUT))):
-            cots[pl.ds(at, n), :, pl.ds(256 * m, COUT)] = w
-
-    place_cot(0, left[64:96], 2)
-    place_cot(130, right[0:32], 2)
-    for b in range(16):
-        place_cot(2 + 8 * b, g_all[:, pl.ds(128 * b, 128)].astype(F32).T, 8)
-
-    @pl.loop(0, 5)
-    def _(n):
-        g = [cots[pl.ds(n * 26 + 2 - kx, 26)].reshape(416, 768) for kx in range(3)]
-        acc = nn(jnp.concatenate(g, 1), conv_t[...])
-        ts = pl.ds(n * 13, 13)
-        d = (acc.reshape(13, 2, 2, H, COUT) * fs[ts]).astype(BF16).astype(F32)
-        for cp in range(2):
-            even, odd = d[:, cp, 0], d[:, cp, 1]
-            for ky, v in enumerate((down(odd), even, odd, up(even))):
-                df[cp, ky, ts] = v
-
-    def window(ky, kx):
-        return df[kx % 2, ky, pl.ds(kx // 2, 64)].reshape(POS, COUT).astype(BF16)
-
-    for ky in (xo, xa, xb, x):
-        for pair in range(2):
-            a, b = [nn(coarse[...], window(ky, kx)) for kx in (2 * pair, 2 * pair + 1)]
-            slabs = (a[:, :128], jnp.concatenate([a[:, 128:], b[:, :64]], 1), b[:, 64:])
-            for n, slab in enumerate(slabs):
-                p = 3 * pair + n
-                part[ky, p] = slab.astype(BF16)
-                if ky is xo:
-                    along_x(xo, p, 1)
-                elif ky is (xa, xb)[p % 2]:
-                    along_x(ky, p, 0)
-
     total = None
     for t in range(16):
         term = nn(window(t // 4, t % 4), own_up[t])
         total = term if total is None else total + term
     c_pos[...] = total
 
-    far_first = sorted(range(nz), key=lambda d: -min(d, nz - d))
     for d in far_first:
         zz = lax.rem(z + d, nz)
         q = second(zz)
@@ -319,78 +313,67 @@
             acc = term if acc is None else acc + term
         r_pos[pl.ds(256 * n, 256), :] = acc + own_bias
 
-    for n in range(4):
+    for n in range(5):
         refine(n)
-
-    half = PIECE // ny
-
-    def part_of(h):
-        return pl.ds(pl.multiple_of(h * half, 16), half)
 
     for d in far_first:
         arrived(rx2.at[d], x2r.at[d])
-        total = kept[d] + rx2[d].astype(F32)
-        kept[d] = total
-        sb2[d] = total.astype(BF16)
-        for f in range(ny - 1, -1, -1):
-            if (d, f) != (0, 0):
-                h = part_of(lax.rem(y + f, ny))
-                send(sb2.at[d, h, :], rz.at[slot(d, f)], zs_s.at[slot(d, f)], zs_r.at[slot(d, f)], zy[d, f])
-    for n in range(4, 8):
+        acc = kept[d] + rx2[d].astype(F32)
+        if d > 0:
+            sb2[d] = acc.astype(BF16)
+            send(sb2.at[d], rz.at[d], zs_s.at[d], zs_r.at[d], zdev[d])
+        else:
+            kept[0] = acc
+    for n in range(5, 8):
         refine(n)
-    for i in range(H):
-        c_grad[i] = c_pos[pl.ds(i, WC, stride=H), :].astype(BF16)
-    mine_rows = part_of(y)
-    acc = kept[0, mine_rows, :]
-    for d, f in links[1:]:
-        arrived(rz.at[slot(d, f)], zs_r.at[slot(d, f)])
-        acc = acc + rz[slot(d, f)].astype(F32)
-    res[x, z, mine_rows, :] = acc.astype(BF16)
-    here = res.at[x, z, mine_rows, :]
-    for d, f in links[:0:-1]:
-        send(here, here, azs.at[slot(d, f)], azr.at[slot(d, f)], zy[d, f])
-
     for r in range(2):
         for i in range(H):
             g32[pl.ds(2 * i + r, OWN_OUT, stride=16), :] = r_pos[pl.ds(8 * r + i, 128, stride=16), :].T
     refined[...] = g32[...].reshape(OWN_OUT, 16, 128).astype(BF16)
-
-    def origin(d, f):
-        return lax.rem(z + nz - d, nz), part_of(lax.rem(y + f, ny))
+    acc = kept[0]
+    for d in near_first[1:]:
+        arrived(rz.at[d], zs_r.at[d])
+        acc = acc + rz[d].astype(F32)
+    ys[...] = acc
+    send(ys, yr, y_sem.at[0], y_sem.at[1], ydev)
+    for i in range(H):
+        c_grad[i] = c_pos[pl.ds(i, WC, stride=H), :].astype(BF16)
+    arrived(yr, y_sem.at[1])
+    res[x, z] = (acc + yr[...]).astype(BF16)
+    here = res.at[x, z]
+    for d in near_first[1:]:
+        send(here, here, azs.at[d], azr.at[d], zdev[d])
 
     def direct(d):
         return d == nz // 2
 
-    def spread_x(d, f):
-        zz, rows = origin(d, f)
-        n = slot(d, f)
-        got = res.at[x, zz, rows, :]
-        if (d, f) != (0, 0):
-            arrived(got, azr.at[n])
+    def spread_x(d):
+        zz = lax.rem(z + nz - d, nz)
+        got = res.at[x, zz]
+        if d > 0:
+            arrived(got, azr.at[d])
         if direct(d):
-            send(got, got, axs.at[2, n], axr.at[2, n], dev(xo, z, y))
-        send(got, got, axs.at[0, n], axr.at[0, n], dev(second(zz), z, y))
-        send(got, got, axs.at[1, n], axr.at[1, n], dev(first(zz), z, y))
-
-    def forward_x(d, f):
-        zz, rows = origin(d, f)
-        n = slot(d, f)
-        got = res.at[second(zz), zz, rows, :]
-        arrived(got, axr.at[0, n])
+            send(got, got, axs.at[2, d], axr.at[2, d], dev(xo, z, y))
+        send(got, got, axs.at[0, d], axr.at[0, d], dev(second(zz), z, y))
+        send(got, got, axs.at[1, d], axr.at[1, d], dev(first(zz), z, y))
+
+    def forward_x(d):
+        zz = lax.rem(z + nz - d, nz)
+        got = res.at[second(zz), zz]
+        arrived(got, axr.at[0, d])
         if not direct(d):
-            send(got, got, axs.at[2, n], axr.at[2, n], dev(first(zz), z, y))
-
-    lag = 4
-    for n in range(len(links) + lag):
-        if n < len(links):
-            spread_x(*links[n])
+            send(got, got, axs.at[2, d], axr.at[2, d], dev(first(zz), z, y))
+
+    lag = 3
+    for n in range(nz + lag):
+        if n < nz:
+            spread_x(near_first[n])
         if n >= lag:
-            forward_x(*links[n - lag])
-    for d, f in links:
-        zz, rows = origin(d, f)
-        n = slot(d, f)
-        arrived(res.at[first(zz), zz, rows, :], axr.at[1, n])
-        arrived(res.at[xo, zz, rows, :], axr.at[2, n])
+            forward_x(near_first[n - lag])
+    for d in near_first:
+        zz = lax.rem(z + nz - d, nz)
+        arrived(res.at[first(zz), zz], axr.at[1, d])
+        arrived(res.at[xo, zz], axr.at[2, d])
     for copy in started:
         copy.wait_send()
 
@@ -439,10 +422,12 @@
             vm((nz, PIECE, 128), BF16),
             vm((nz, PIECE, 128), BF16),
             vm((nz, PIECE, 128), BF16),
-            vm((nz * ny, PIECE // ny, 128), BF16),
+            vm((nz, PIECE, 128), BF16),
+            vm((PIECE, 128), F32),
+            vm((PIECE, 128), F32),
             dma((4,)), dma((3,)), dma((3,)), dma((3, PIECES)), dma((3, PIECES)), dma((2, 4)), dma((2, 4)),
-            dma((nz, 2)), dma((nz, 2)), dma((nz,)), dma((nz,)), dma((nz * ny,)), dma((nz * ny,)),
-            dma((nz * ny,)), dma((nz * ny,)), dma((3, nz * ny)), dma((3, nz * ny)),
+            dma((nz, 2)), dma((nz, 2)), dma((nz,)), dma((nz,)), dma((nz,)), dma((nz,)), dma((2,)),
+            dma((nz,)), dma((nz,)), dma((3, nz)), dma((3, nz)),
         ],
         compiler_params=pltpu.CompilerParams(
             collective_id=0, has_side_effects=True, vmem_limit_bytes=LIMIT
@@ -451,15 +436,19 @@
     )(*args)
 
 
-def unpack_kernel(refined, c_grad, sums, refined_out, c_out, up_grad, conv_grad, src, up, conv, sems, out_sems):
+def unpack_kernel(refined, c_grad, sums, refined_out, c_out, up_grad, conv_grad, ref, cg, src, up, conv, sems, out_sems):
     nx = sums.shape[0]
+    loads = [pltpu.make_async_copy(sums.at[k], src.at[k], sems.at[k]) for k in range(nx)]
+    loads += [
+        pltpu.make_async_copy(refined, ref, sems.at[nx]),
+        pltpu.make_async_copy(c_grad, cg, sems.at[nx + 1]),
+    ]
+    for copy in loads:
+        copy.start()
     passes = [
-        pltpu.make_async_copy(refined, refined_out, out_sems.at[nx]),
-        pltpu.make_async_copy(c_grad, c_out, out_sems.at[nx + 1]),
+        pltpu.make_async_copy(ref, refined_out, out_sems.at[nx]),
+        pltpu.make_async_copy(cg, c_out, out_sems.at[nx + 1]),
     ]
-    loads = [pltpu.make_async_copy(sums.at[k], src.at[k], sems.at[k]) for k in range(nx)]
-    for copy in loads + passes:
-        copy.start()
     for ky in range(4):
         loads[ky].wait()
         for pair in range(2):
@@ -469,6 +458,10 @@
         copy = pltpu.make_async_copy(up.at[ky], up_grad.at[ky], out_sems.at[ky])
         copy.start()
         passes.append(copy)
+
+    for load, copy in zip(loads[nx:], passes):
+        load.wait()
+        copy.start()
 
     def block(b):
         return src[b // 4, 6 + b % 4 // 2, pl.ds(b % 2 * OWN_OUT, OWN_OUT), :].astype(F32)
@@ -497,10 +490,12 @@
         in_specs=[any_] * 3,
         out_specs=[any_] * 4,
         scratch_shapes=[
+            pltpu.VMEM(refined.shape, BF16),
+            pltpu.VMEM(c_grad.shape, BF16),
             pltpu.VMEM(sums.shape, BF16),
             pltpu.VMEM(up, F32),
             pltpu.VMEM(conv, F32),
-            pltpu.SemaphoreType.DMA((4,)),
+            pltpu.SemaphoreType.DMA((6,)),
             pltpu.SemaphoreType.DMA((7,)),
         ],
         compiler_params=pltpu.CompilerParams(vmem_limit_bytes=LIMIT),

time: 76.9 us -> 67.7 us (0.88); the launches traced: 75.7 us -> 67.3 us
  Pallas kernels: 74.9 us -> 66.5 us
    pallas_call x1, Pallas kernels: 11.1 us -> 2.52 us  [unpack(): pl.pallas_call(unpack_kernel, out_shape=(jax.ShapeDtypeStruct(refined.sha...]
where the time goes in v4:
time: 67.7 us; the launch traced here: 67.3 us
  Pallas kernels  66.5 us (98%)
  between operations  0.8 us (1%)
    pallas_call x1, Pallas kernels, strip(): pl.pallas_call(functools.partial(kernel, dims), out_shape=(jax.ShapeDtype...  64 us
    pallas_call x1, Pallas kernels, unpack(): pl.pallas_call(unpack_kernel, out_shape=(jax.ShapeDtypeStruct(refined.sha...  2.52 us

profile of v4, /device:TPU:2, one launch (start us, length us, event | category | flops | bytes accessed | tf_op | source)
XLA Modules:
  0.0 67.3 jit_solution(1838336189312172968)
XLA Ops:
  0.6 64.0 %strip.1 = (bf16[48,16,128]{2,1,0:T(8,128)(2,1)}, bf16[8,64,96]{2,1,0:T(8,128)(2,1)}, bf16[4,8,96,128]{3,2,1,0:T(8,128)(2,1)}) custom-call(bf16[8,64,96]{2,1,0:T(8,128)(2,1)} %bitcast.7, bf16[48,16,128]{2,1,0:T(8,128)(2,1)} %cot_hbm.1, bf16[4,4,192,384]{3,2,1,0:T(8,128)(2,1)} %bitcast.6, bf16[3,3,192,192]{3,2,1,0:T(8,128)(2,1)} %conv_hbm.1, ...), custom_call_target="tpu_custom_call" | custom-call | tf_op jit(solution)/shard_map/strip/pallas_call | solution.py:386
  64.6 2.5 %unpack.1 = (bf16[48,16,128]{2,1,0:T(8,128)(2,1)}, bf16[8,64,96]{2,1,0:T(8,128)(2,1)}, f32[4,4,96,192]{3,2,1,0:T(8,128)}, f32[3,3,48,192]{3,2,1,0:T(8,128)}) custom-call(bf16[48,16,128]{2,1,0:T(8,128)(2,1)} %get-tuple-element.11.refined, bf16[8,64,96]{2,1,0:T(8,128)(2,1)} %get-tuple-element.12.c_grad, bf16[4,8,96,128]{3,2,1,0:T(8,128)(2,1)} %get-tuple-element.13.sums), custom_call_target="tpu_custom_call" | custom-call | tf_op jit(solution)/shard_map/unpack/pallas_call | solution.py:482

commit v5 on v4

--- a/solution.py
+++ b/solution.py
@@ -46,7 +46,7 @@
 
 def kernel(dims, coarse_hbm, cot_hbm, up_hbm, conv_hbm, up_b, conv_b,
            refined, c_grad, res,
-           coarse_in, cot_in, coarse, cot, edge, g32, c_all, g_all, e_all, up_w, conv_w, conv_t, mine, own_up,
+           coarse_in, cot_in, coarse, cot, c_end, g_end, g32, c_all, g_all, ce_all, ge_all, up_w, conv_w, conv_t, mine, own_up,
            xf, xl, pre, fs, hid, cots, df, part, r_pos, c_pos,
            rx1, kept, sb1, rx2, sb2, rz, ys, yr,
            w_sem, cs, cr, gs, gr, es, er, x1s, x1r, x2s, x2r, zs_s, zs_r, y_sem,
@@ -98,6 +98,8 @@
         c_pos[pl.ds(i, WC, stride=H), :] = coarse_in[i].astype(F32)
     for n in range(4):
         coarse[:, pl.ds(128 * n, 128)] = c_pos[pl.ds(128 * n, 128), :].T.astype(BF16)
+    c_end[0] = c_pos[pl.ds(POS - 16, 16), :].astype(BF16)
+    c_end[1] = c_pos[pl.ds(0, 16), :].astype(BF16)
     pl.semaphore_wait(barrier, len(greet))
 
     started = []
@@ -123,10 +125,11 @@
     def g_block(r, k):
         return g_all.at[pl.ds(pl.multiple_of(r * OWN_OUT, 16), OWN_OUT), pl.ds(k * width, width)]
 
-    def e_block(n, r):
-        return e_all.at[n, pl.ds(pl.multiple_of(r * OWN_OUT, 16), OWN_OUT), :]
-
     send(coarse, c_block(rank), cs.at[0], cr.at[0], (lon, cross))
+    for n, side in enumerate(sides):
+        for d in range(4):
+            to = (side, lax.rem(rank + d, 4))
+            send(c_end.at[n], ce_all.at[n, rank], es.at[0, n, d], er.at[0, n, d], to)
     send(coarse, c_block(rank), cs.at[1], cr.at[1], (lon, sib))
     loads[1].wait()
     g32[...] = cot_in[...].astype(F32).reshape(OWN_OUT * 16, 128)
@@ -135,18 +138,16 @@
             r_pos[pl.ds(8 * r + i, 128, stride=16), :] = g32[pl.ds(2 * i + r, OWN_OUT, stride=16), :].T
     for n in range(16):
         cot[:, pl.ds(128 * n, 128)] = r_pos[pl.ds(128 * n, 128), :].T.astype(BF16)
-    ends = []
-    for c0, g0 in ((0, 0), (POS - 16, FINE - 32)):
-        c_end = coarse[:, pl.ds(c0, 16)].astype(F32)
-        ends += [cot[:, pl.ds(g0, 32)].astype(F32), c_end[:OWN_OUT], c_end[OWN_OUT:]]
-    edge[...] = jnp.concatenate(ends, 1).astype(BF16)
-    for n, side in enumerate(sides):
-        for d in range(4):
-            send(edge, e_block(n, rank), es.at[n, d], er.at[n, d], (side, lax.rem(rank + d, 4)))
+    g_end[0] = r_pos[pl.ds(FINE - 32, 32), :].astype(BF16)
+    g_end[1] = r_pos[pl.ds(0, 32), :].astype(BF16)
     for k in range(PIECES):
         own_part = cot.at[:, pl.ds(k * width, width)]
         send(own_part, g_block(rank, k), gs.at[0, k], gr.at[0, k], (lon, cross))
         send(own_part, g_block(rank, k), gs.at[1, k], gr.at[1, k], (lon, sib))
+    for n, side in enumerate(sides):
+        for d in range(4):
+            to = (side, lax.rem(rank + d, 4))
+            send(g_end.at[n], ge_all.at[n, rank], es.at[1, n, d], er.at[1, n, d], to)
     c_all[pl.ds(pl.multiple_of(rank * OWN_IN, 16), OWN_IN), :] = coarse[...]
     g_all[pl.ds(pl.multiple_of(rank * OWN_OUT, 16), OWN_OUT), :] = cot[...]
 
@@ -170,10 +171,6 @@
         w = conv_w[t // 3, t % 3]
         mine[t] = nn(w, pick).astype(BF16)
         conv_t[pl.ds(768 * (t % 3) + 256 * (2 - t // 3), COUT), :] = w.astype(F32).T.astype(BF16)
-    src = lax.broadcasted_iota(jnp.int32, (COUT, CIN), 0)
-    dst = lax.broadcasted_iota(jnp.int32, (COUT, CIN), 1)
-    place = src // OWN_OUT * OWN_IN + lax.rem(src, OWN_OUT)
-    spread = [(dst == place + OWN_OUT * h).astype(F32).astype(BF16) for h in range(2)]
 
     arrived(c_block(cross), cr.at[0])
     send(c_block(cross), c_block(cross), cs.at[2], cr.at[2], (lon, sib))
@@ -184,18 +181,16 @@
         own_up[t] = nn(up_w[t // 4, t % 4], pick).astype(BF16)
     for n in range(2):
         for d in range(4):
-            arrived(e_block(n, lax.rem(rank + 4 - d, 4)), er.at[n, d])
+            arrived(ce_all.at[n, lax.rem(rank + 4 - d, 4)], er.at[0, n, d])
     arrived(c_block(sib), cr.at[1])
     arrived(c_block(diag), cr.at[2])
     for b in range(4):
         xf[pl.ds(1 + 16 * b, 16)] = c_all[:, pl.ds(128 * b, 128)].astype(F32).T.reshape(16, H, CIN)
-    left, right = e_all[0].astype(F32).T, e_all[1].astype(F32).T
-
-    def widen(pair):
-        return nn(pair[:16].astype(BF16), spread[0]) + nn(pair[16:].astype(BF16), spread[1])
-
-    xf[0] = widen(left[96:128])[8:]
-    xf[65] = widen(right[32:64])[:8]
+    left, right = [
+        jnp.concatenate([ce_all[n, r].astype(F32) for r in range(4)], 1) for n in range(2)
+    ]
+    xf[0] = left[8:]
+    xf[65] = right[:8]
     xf[66:68] = jnp.zeros((2, H, CIN), F32)
 
     @pl.loop(0, 3)
@@ -214,13 +209,11 @@
             w = jnp.concatenate([up_w[ky, cp + 2 * d] for ky in taps for d in range(2)], 1)
             val = nt(xl[:, pl.ds(rp * 2 * CIN, 4 * CIN)], w)
             pre[:, cp, rp] = val.reshape(66, H, COUT)
-            if (rp, cp) != (1, 1):
-                pass_on(1 + 2 * rp + cp)
+        pass_on(1 + rp)
 
     bias = up_b[...].reshape(1, 1, 1, 1, COUT)
 
-    @pl.loop(0, 22)
-    def _(n):
+    def activate(n):
         ts = pl.ds(n * 3, 3)
         v = pre[ts] + bias
         s = jax.nn.sigmoid(v)
@@ -229,6 +222,10 @@
         for m, w in enumerate(shifted(h)):
             hid[m, pl.ds(n * 6, 6)] = w
 
+    pl.loop(0, 11)(activate)
+    pass_on(3)
+    pl.loop(11, 22)(activate)
+
     def along_x(chunk, p, which):
         send(part.at[chunk, p], rx1.at[p, which], x1s.at[p, which], x1r.at[p, which],
              dev(first(p), z, y))
@@ -237,19 +234,23 @@
         for m, w in enumerate(shifted(v.reshape(n, 2, H, COUT))):
             cots[pl.ds(at, n), :, pl.ds(256 * m, COUT)] = w
 
-    place_cot(0, left[64:96], 2)
-    place_cot(130, right[0:32], 2)
-    cols = 2 * WC // PIECES
     for k in range(PIECES):
         arrived(g_block(sib, k), gr.at[1, k])
         arrived(g_block(diag, k), gr.at[2, k])
-        for b in range(k * cols // 8, (k + 1) * cols // 8):
-            place_cot(2 + 8 * b, g_all[:, pl.ds(128 * b, 128)].astype(F32).T, 8)
-        count = cols + 2 * (k == PIECES - 1)
-        g = [cots[pl.ds(k * cols + 2 - kx, count)].reshape(16 * count, 768) for kx in range(3)]
+    for b in range(16):
+        place_cot(2 + 8 * b, g_all[:, pl.ds(128 * b, 128)].astype(F32).T, 8)
+    for n in range(2):
+        for d in range(4):
+            arrived(ge_all.at[n, lax.rem(rank + 4 - d, 4)], er.at[1, n, d])
+        both = jnp.concatenate([ge_all[n, r].astype(F32) for r in range(4)], 1)
+        place_cot(130 * n, both, 2)
+
+    @pl.loop(0, 5)
+    def _(n):
+        g = [cots[pl.ds(n * 26 + 2 - kx, 26)].reshape(416, 768) for kx in range(3)]
         acc = nn(jnp.concatenate(g, 1), conv_t[...])
-        ts = pl.ds(k * cols // 2, count // 2)
-        d = (acc.reshape(count // 2, 2, 2, H, COUT) * fs[ts]).astype(BF16).astype(F32)
+        ts = pl.ds(n * 13, 13)
+        d = (acc.reshape(13, 2, 2, H, COUT) * fs[ts]).astype(BF16).astype(F32)
         for cp in range(2):
             even, odd = d[:, cp, 0], d[:, cp, 1]
             for ky, v in enumerate((down(odd), even, odd, up(even))):
@@ -397,11 +398,13 @@
             vm((OWN_OUT, 2 * H, 2 * WC), BF16),
             vm((OWN_IN, POS), BF16),
             vm((OWN_OUT, FINE), BF16),
-            vm((OWN_OUT, 128), BF16),
+            vm((2, 16, OWN_IN), BF16),
+            vm((2, 32, OWN_OUT), BF16),
             vm((OWN_OUT * 2 * H, 2 * WC), F32),
             vm((CIN, POS), BF16),
             vm((COUT, FINE), BF16),
-            vm((2, COUT, 128), BF16),
+            vm((2, 4, 16, OWN_IN), BF16),
+            vm((2, 4, 32, OWN_OUT), BF16),
             vm((4, 4, COUT, CIN), BF16),
             vm((3, 3, COUT, COUT), BF16),
             vm((9 * 256, COUT), BF16),
@@ -425,7 +428,7 @@
             vm((nz, PIECE, 128), BF16),
             vm((PIECE, 128), F32),
             vm((PIECE, 128), F32),
-            dma((4,)), dma((3,)), dma((3,)), dma((3, PIECES)), dma((3, PIECES)), dma((2, 4)), dma((2, 4)),
+            dma((4,)), dma((3,)), dma((3,)), dma((3, PIECES)), dma((3, PIECES)), dma((2, 2, 4)), dma((2, 2, 4)),
             dma((nz, 2)), dma((nz, 2)), dma((nz,)), dma((nz,)), dma((nz,)), dma((nz,)), dma((2,)),
             dma((nz,)), dma((nz,)), dma((3, nz)), dma((3, nz)),
         ],

time: 67.7 us -> 63.7 us (0.941)
  Pallas kernels: 66.5 us -> 62.5 us
    pallas_call x1, Pallas kernels: 64 us -> 60 us  [strip(): pl.pallas_call(functools.partial(kernel, dims), out_shape=(jax.ShapeDtype...]
where the time goes in v5:
time: 63.7 us; the launch traced here: 63.3 us
  Pallas kernels  62.5 us (98%)
  between operations  0.8 us (1%)
    pallas_call x1, Pallas kernels, strip(): pl.pallas_call(functools.partial(kernel, dims), out_shape=(jax.ShapeDtype...  60 us
    pallas_call x1, Pallas kernels, unpack(): pl.pallas_call(unpack_kernel, out_shape=(jax.ShapeDtypeStruct(refined.sha...  2.52 us

profile of v5, /device:TPU:2, one launch (start us, length us, event | category | flops | bytes accessed | tf_op | source)
XLA Modules:
  0.0 63.3 jit_solution(14900288873995267838)
XLA Ops:
  0.6 60.0 %strip.1 = (bf16[48,16,128]{2,1,0:T(8,128)(2,1)}, bf16[8,64,96]{2,1,0:T(8,128)(2,1)}, bf16[4,8,96,128]{3,2,1,0:T(8,128)(2,1)}) custom-call(bf16[8,64,96]{2,1,0:T(8,128)(2,1)} %bitcast.7, bf16[48,16,128]{2,1,0:T(8,128)(2,1)} %cot_hbm.1, bf16[4,4,192,384]{3,2,1,0:T(8,128)(2,1)} %bitcast.6, bf16[3,3,192,192]{3,2,1,0:T(8,128)(2,1)} %conv_hbm.1, ...), custom_call_target="tpu_custom_call" | custom-call | tf_op jit(solution)/shard_map/strip/pallas_call | solution.py:387
  60.6 2.5 %unpack.1 = (bf16[48,16,128]{2,1,0:T(8,128)(2,1)}, bf16[8,64,96]{2,1,0:T(8,128)(2,1)}, f32[4,4,96,192]{3,2,1,0:T(8,128)}, f32[3,3,48,192]{3,2,1,0:T(8,128)}) custom-call(bf16[48,16,128]{2,1,0:T(8,128)(2,1)} %get-tuple-element.11.refined, bf16[8,64,96]{2,1,0:T(8,128)(2,1)} %get-tuple-element.12.c_grad, bf16[4,8,96,128]{3,2,1,0:T(8,128)(2,1)} %get-tuple-element.13.sums), custom_call_target="tpu_custom_call" | custom-call | tf_op jit(solution)/shard_map/unpack/pallas_call | solution.py:485

commit v6 on v5

--- a/solution.py
+++ b/solution.py
@@ -138,16 +138,18 @@
             r_pos[pl.ds(8 * r + i, 128, stride=16), :] = g32[pl.ds(2 * i + r, OWN_OUT, stride=16), :].T
     for n in range(16):
         cot[:, pl.ds(128 * n, 128)] = r_pos[pl.ds(128 * n, 128), :].T.astype(BF16)
-    g_end[0] = r_pos[pl.ds(FINE - 32, 32), :].astype(BF16)
-    g_end[1] = r_pos[pl.ds(0, 32), :].astype(BF16)
+    gap = jnp.zeros((16, 64 - OWN_OUT), F32)
+    for n, at in enumerate((FINE - 32, 0)):
+        two = [r_pos[pl.ds(at, 16), :], gap, r_pos[pl.ds(at + 16, 16), :], gap]
+        g_end[n] = jnp.concatenate(two, 1).astype(BF16)
+    for n, side in enumerate(sides):
+        for d in range(4):
+            to = (side, lax.rem(rank + d, 4))
+            send(g_end.at[n], ge_all.at[n, rank], es.at[1, n, d], er.at[1, n, d], to)
     for k in range(PIECES):
         own_part = cot.at[:, pl.ds(k * width, width)]
         send(own_part, g_block(rank, k), gs.at[0, k], gr.at[0, k], (lon, cross))
         send(own_part, g_block(rank, k), gs.at[1, k], gr.at[1, k], (lon, sib))
-    for n, side in enumerate(sides):
-        for d in range(4):
-            to = (side, lax.rem(rank + d, 4))
-            send(g_end.at[n], ge_all.at[n, rank], es.at[1, n, d], er.at[1, n, d], to)
     c_all[pl.ds(pl.multiple_of(rank * OWN_IN, 16), OWN_IN), :] = coarse[...]
     g_all[pl.ds(pl.multiple_of(rank * OWN_OUT, 16), OWN_OUT), :] = cot[...]
 
@@ -234,19 +236,22 @@
         for m, w in enumerate(shifted(v.reshape(n, 2, H, COUT))):
             cots[pl.ds(at, n), :, pl.ds(256 * m, COUT)] = w
 
-    for k in range(PIECES):
+    def place_edge(n):
+        for d in range(4):
+            arrived(ge_all.at[n, lax.rem(rank + 4 - d, 4)], er.at[1, n, d])
+        cols = []
+        for h in (0, 64):
+            block = [ge_all[n, r][:, h:h + OWN_OUT].astype(F32) for r in range(4)]
+            cols.append(jnp.concatenate(block, 1))
+        place_cot(130 * n, jnp.concatenate(cols, 0), 2)
+
+    def place_piece(k):
         arrived(g_block(sib, k), gr.at[1, k])
         arrived(g_block(diag, k), gr.at[2, k])
-    for b in range(16):
-        place_cot(2 + 8 * b, g_all[:, pl.ds(128 * b, 128)].astype(F32).T, 8)
-    for n in range(2):
-        for d in range(4):
-            arrived(ge_all.at[n, lax.rem(rank + 4 - d, 4)], er.at[1, n, d])
-        both = jnp.concatenate([ge_all[n, r].astype(F32) for r in range(4)], 1)
-        place_cot(130 * n, both, 2)
-
-    @pl.loop(0, 5)
-    def _(n):
+        for b in range(4 * k, 4 * k + 4):
+            place_cot(2 + 8 * b, g_all[:, pl.ds(128 * b, 128)].astype(F32).T, 8)
+
+    def adjoint(n):
         g = [cots[pl.ds(n * 26 + 2 - kx, 26)].reshape(416, 768) for kx in range(3)]
         acc = nn(jnp.concatenate(g, 1), conv_t[...])
         ts = pl.ds(n * 13, 13)
@@ -255,6 +260,15 @@
             even, odd = d[:, cp, 0], d[:, cp, 1]
             for ky, v in enumerate((down(odd), even, odd, up(even))):
                 df[cp, ky, ts] = v
+
+    place_edge(0)
+    place_piece(0)
+    place_piece(1)
+    pl.loop(0, 2)(adjoint)
+    place_edge(1)
+    place_piece(2)
+    place_piece(3)
+    pl.loop(2, 5)(adjoint)
 
     def window(ky, kx):
         return df[kx % 2, ky, pl.ds(kx // 2, 64)].reshape(POS, COUT).astype(BF16)
@@ -292,12 +306,6 @@
         along_x(xo, p, 1)
         along_x(first(p), p, 0)
 
-    total = None
-    for t in range(16):
-        term = nn(window(t // 4, t % 4), own_up[t])
-        total = term if total is None else total + term
-    c_pos[...] = total
-
     for d in far_first:
         zz = lax.rem(z + d, nz)
         q = second(zz)
@@ -307,6 +315,12 @@
         sb1[d] = (part[q, zz].astype(F32) + rx1[zz, 1].astype(F32)).astype(BF16)
         send(sb1.at[d], rx2.at[d], x2s.at[d], x2r.at[d], dev(q, z, y))
 
+    total = None
+    for t in range(16):
+        term = nn(window(t // 4, t % 4), own_up[t])
+        total = term if total is None else total + term
+    c_pos[...] = total
+
     def refine(n):
         acc = None
         for t in range(9):
@@ -314,7 +328,7 @@
             acc = term if acc is None else acc + term
         r_pos[pl.ds(256 * n, 256), :] = acc + own_bias
 
-    for n in range(5):
+    for n in range(4):
         refine(n)
 
     for d in far_first:
@@ -325,7 +339,7 @@
             send(sb2.at[d], rz.at[d], zs_s.at[d], zs_r.at[d], zdev[d])
         else:
             kept[0] = acc
-    for n in range(5, 8):
+    for n in range(4, 8):
         refine(n)
     for r in range(2):
         for i in range(H):
@@ -399,12 +413,12 @@
             vm((OWN_IN, POS), BF16),
             vm((OWN_OUT, FINE), BF16),
             vm((2, 16, OWN_IN), BF16),
-            vm((2, 32, OWN_OUT), BF16),
+            vm((2, 16, 128), BF16),
             vm((OWN_OUT * 2 * H, 2 * WC), F32),
             vm((CIN, POS), BF16),
             vm((COUT, FINE), BF16),
             vm((2, 4, 16, OWN_IN), BF16),
-            vm((2, 4, 32, OWN_OUT), BF16),
+            vm((2, 4, 16, 128), BF16),
             vm((4, 4, COUT, CIN), BF16),
             vm((3, 3, COUT, COUT), BF16),
             vm((9 * 256, COUT), BF16),

time: 63.7 us -> 63.6 us (level)
  no operation moved by 1% of the time
where the time goes in v6:
time: 63.6 us; the launch traced here: 63.1 us
  Pallas kernels  62.3 us (98%)
  between operations  0.8 us (1%)
    pallas_call x1, Pallas kernels, strip(): pl.pallas_call(functools.partial(kernel, dims), out_shape=(jax.ShapeDtype...  59.8 us
    pallas_call x1, Pallas kernels, unpack(): pl.pallas_call(unpack_kernel, out_shape=(jax.ShapeDtypeStruct(refined.sha...  2.52 us

profile of v6, /device:TPU:2, one launch (start us, length us, event | category | flops | bytes accessed | tf_op | source)
XLA Modules:
  0.0 63.1 jit_solution(3190138136504958662)
XLA Ops:
  0.6 59.8 %strip.1 = (bf16[48,16,128]{2,1,0:T(8,128)(2,1)}, bf16[8,64,96]{2,1,0:T(8,128)(2,1)}, bf16[4,8,96,128]{3,2,1,0:T(8,128)(2,1)}) custom-call(bf16[8,64,96]{2,1,0:T(8,128)(2,1)} %bitcast.7, bf16[48,16,128]{2,1,0:T(8,128)(2,1)} %cot_hbm.1, bf16[4,4,192,384]{3,2,1,0:T(8,128)(2,1)} %bitcast.6, bf16[3,3,192,192]{3,2,1,0:T(8,128)(2,1)} %conv_hbm.1, ...), custom_call_target="tpu_custom_call" | custom-call | tf_op jit(solution)/shard_map/strip/pallas_call | solution.py:401
  60.4 2.5 %unpack.1 = (bf16[48,16,128]{2,1,0:T(8,128)(2,1)}, bf16[8,64,96]{2,1,0:T(8,128)(2,1)}, f32[4,4,96,192]{3,2,1,0:T(8,128)}, f32[3,3,48,192]{3,2,1,0:T(8,128)}) custom-call(bf16[48,16,128]{2,1,0:T(8,128)(2,1)} %get-tuple-element.11.refined, bf16[8,64,96]{2,1,0:T(8,128)(2,1)} %get-tuple-element.12.c_grad, bf16[4,8,96,128]{3,2,1,0:T(8,128)(2,1)} %get-tuple-element.13.sums), custom_call_target="tpu_custom_call" | custom-call | tf_op jit(solution)/shard_map/unpack/pallas_call | solution.py:499

commit v7 on v6

--- a/solution.py
+++ b/solution.py
@@ -46,7 +46,7 @@
 
 def kernel(dims, coarse_hbm, cot_hbm, up_hbm, conv_hbm, up_b, conv_b,
            refined, c_grad, res,
-           coarse_in, cot_in, coarse, cot, c_end, g_end, g32, c_all, g_all, ce_all, ge_all, up_w, conv_w, conv_t, mine, own_up,
+           coarse_in, cot_in, coarse, cot, cot3, c_end, g_end, g32, c_all, g_all, ce_all, ge_all, up_w, conv_w, conv_t, mine, own_up,
            xf, xl, pre, fs, hid, cots, df, part, r_pos, c_pos,
            rx1, kept, sb1, rx2, sb2, rz, ys, yr,
            w_sem, cs, cr, gs, gr, es, er, x1s, x1r, x2s, x2r, zs_s, zs_r, y_sem,
@@ -161,6 +161,19 @@
     for m in range(3):
         cots[:, :, pl.ds(256 * m + COUT, 64)] = pad
     conv_t[...] = jnp.zeros(conv_t.shape, BF16)
+    cot3[pl.ds(OWN_OUT, OWN_OUT), :] = cot[...]
+    for m in (0, 2):
+        for r in range(2):
+            for i in range(H):
+                p = 2 * i + r + m - 1
+                rows = pl.ds(8 * r + i, 128, stride=16)
+                if 0 <= p < 16:
+                    r_pos[rows, :] = g32[pl.ds(p, OWN_OUT, stride=16), :].T
+                else:
+                    r_pos[rows, :] = jnp.zeros((128, OWN_OUT), F32)
+        for n in range(16):
+            cot3[pl.ds(OWN_OUT * m, OWN_OUT), pl.ds(128 * n, 128)] = r_pos[pl.ds(128 * n, 128), :].T.astype(BF16)
+
     for load in loads[2:]:
         load.wait()
     own_bias = jnp.zeros((1, OWN_OUT), F32)
@@ -232,6 +245,28 @@
         send(part.at[chunk, p], rx1.at[p, which], x1s.at[p, which], x1r.at[p, which],
              dev(first(p), z, y))
 
+    def spot(b):
+        return b // 4, 6 + b % 4 // 2, pl.ds(b % 2 * OWN_OUT, OWN_OUT)
+
+    def put(b, v):
+        c, p, rows = spot(b)
+        part[c, p, rows, :] = v.astype(BF16)
+
+    tails = []
+    taps = [nn(cot3[...], hid[1, pl.ds(kx, 128)].reshape(FINE, COUT)) for kx in range(3)]
+    for t in range(9):
+        g = taps[t % 3][OWN_OUT * (2 - t // 3):OWN_OUT * (3 - t // 3)]
+        put(t, g[:, :128])
+        tails.append(g[:, 128:])
+    tails.append(jnp.zeros((OWN_OUT, 64), F32))
+    for u in range(5):
+        put(9 + u, jnp.concatenate(tails[2 * u:2 * u + 2], 1))
+    for b in (14, 15):
+        put(b, jnp.zeros((OWN_OUT, 128), F32))
+    for p in (6, 7):
+        along_x(xo, p, 1)
+        along_x(first(p), p, 0)
+
     def place_cot(at, v, n):
         for m, w in enumerate(shifted(v.reshape(n, 2, H, COUT))):
             cots[pl.ds(at, n), :, pl.ds(256 * m, COUT)] = w
@@ -285,27 +320,6 @@
                 elif ky is (xa, xb)[p % 2]:
                     along_x(ky, p, 0)
 
-    def spot(b):
-        return b // 4, 6 + b % 4 // 2, pl.ds(b % 2 * OWN_OUT, OWN_OUT)
-
-    def put(b, v):
-        c, p, rows = spot(b)
-        part[c, p, rows, :] = v.astype(BF16)
-
-    tails = []
-    for t in range(9):
-        g = nn(cot[...], hid[t // 3, pl.ds(t % 3, 128)].reshape(FINE, COUT))
-        put(t, g[:, :128])
-        tails.append(g[:, 128:])
-    tails.append(jnp.zeros((OWN_OUT, 64), F32))
-    for u in range(5):
-        put(9 + u, jnp.concatenate(tails[2 * u:2 * u + 2], 1))
-    for b in (14, 15):
-        put(b, jnp.zeros((OWN_OUT, 128), F32))
-    for p in (6, 7):
-        along_x(xo, p, 1)
-        along_x(first(p), p, 0)
-
     for d in far_first:
         zz = lax.rem(z + d, nz)
         q = second(zz)
@@ -341,18 +355,12 @@
             kept[0] = acc
     for n in range(4, 8):
         refine(n)
-    for r in range(2):
-        for i in range(H):
-            g32[pl.ds(2 * i + r, OWN_OUT, stride=16), :] = r_pos[pl.ds(8 * r + i, 128, stride=16), :].T
-    refined[...] = g32[...].reshape(OWN_OUT, 16, 128).astype(BF16)
     acc = kept[0]
     for d in near_first[1:]:
         arrived(rz.at[d], zs_r.at[d])
         acc = acc + rz[d].astype(F32)
     ys[...] = acc
     send(ys, yr, y_sem.at[0], y_sem.at[1], ydev)
-    for i in range(H):
-        c_grad[i] = c_pos[pl.ds(i, WC, stride=H), :].astype(BF16)
     arrived(yr, y_sem.at[1])
     res[x, z] = (acc + yr[...]).astype(BF16)
     here = res.at[x, z]
@@ -383,6 +391,13 @@
     for n in range(nz + lag):
         if n < nz:
             spread_x(near_first[n])
+        if n == 0:
+            for r in range(2):
+                for i in range(H):
+                    g32[pl.ds(2 * i + r, OWN_OUT, stride=16), :] = r_pos[pl.ds(8 * r + i, 128, stride=16), :].T
+            refined[...] = g32[...].reshape(OWN_OUT, 16, 128).astype(BF16)
+            for i in range(H):
+                c_grad[i] = c_pos[pl.ds(i, WC, stride=H), :].astype(BF16)
         if n >= lag:
             forward_x(near_first[n - lag])
     for d in near_first:
@@ -412,6 +427,7 @@
             vm((OWN_OUT, 2 * H, 2 * WC), BF16),
             vm((OWN_IN, POS), BF16),
             vm((OWN_OUT, FINE), BF16),
+            vm((3 * OWN_OUT, FINE), BF16),
             vm((2, 16, OWN_IN), BF16),
             vm((2, 16, 128), BF16),
             vm((OWN_OUT * 2 * H, 2 * WC), F32),

time: 63.6 us -> 62.8 us (0.987)
  no operation moved by 1% of the time
where the time goes in v7:
time: 62.8 us; the launch traced here: 62.6 us
  Pallas kernels  61.8 us (98%)
  between operations  0.8 us (1%)
    pallas_call x1, Pallas kernels, strip(): pl.pallas_call(functools.partial(kernel, dims), out_shape=(jax.ShapeDtype...  59.3 us
    pallas_call x1, Pallas kernels, unpack(): pl.pallas_call(unpack_kernel, out_shape=(jax.ShapeDtypeStruct(refined.sha...  2.52 us

profile of v7, /device:TPU:2, one launch (start us, length us, event | category | flops | bytes accessed | tf_op | source)
XLA Modules:
  0.0 62.6 jit_solution(1391908591168694232)
XLA Ops:
  0.6 59.3 %strip.1 = (bf16[48,16,128]{2,1,0:T(8,128)(2,1)}, bf16[8,64,96]{2,1,0:T(8,128)(2,1)}, bf16[4,8,96,128]{3,2,1,0:T(8,128)(2,1)}) custom-call(bf16[8,64,96]{2,1,0:T(8,128)(2,1)} %bitcast.7, bf16[48,16,128]{2,1,0:T(8,128)(2,1)} %cot_hbm.1, bf16[4,4,192,384]{3,2,1,0:T(8,128)(2,1)} %bitcast.6, bf16[3,3,192,192]{3,2,1,0:T(8,128)(2,1)} %conv_hbm.1, ...), custom_call_target="tpu_custom_call" | custom-call | tf_op jit(solution)/shard_map/strip/pallas_call | solution.py:416
  59.9 2.5 %unpack.1 = (bf16[48,16,128]{2,1,0:T(8,128)(2,1)}, bf16[8,64,96]{2,1,0:T(8,128)(2,1)}, f32[4,4,96,192]{3,2,1,0:T(8,128)}, f32[3,3,48,192]{3,2,1,0:T(8,128)}) custom-call(bf16[48,16,128]{2,1,0:T(8,128)(2,1)} %get-tuple-element.11.refined, bf16[8,64,96]{2,1,0:T(8,128)(2,1)} %get-tuple-element.12.c_grad, bf16[4,8,96,128]{3,2,1,0:T(8,128)(2,1)} %get-tuple-element.13.sums), custom_call_target="tpu_custom_call" | custom-call | tf_op jit(solution)/shard_map/unpack/pallas_call | solution.py:515

commit v8 on v7

--- a/solution.py
+++ b/solution.py
@@ -179,21 +179,12 @@
     own_bias = jnp.zeros((1, OWN_OUT), F32)
     for r in range(4):
         own_bias += jnp.where(rank == r, conv_b[:, pl.ds(OWN_OUT * r, OWN_OUT)], 0.0)
-    a_of = lax.broadcasted_iota(jnp.int32, (COUT, OWN_OUT), 0)
-    b_of = lax.broadcasted_iota(jnp.int32, (COUT, OWN_OUT), 1)
-    pick = (a_of == b_of + OWN_OUT * rank).astype(F32).astype(BF16)
     for t in range(9):
         w = conv_w[t // 3, t % 3]
-        mine[t] = nn(w, pick).astype(BF16)
         conv_t[pl.ds(768 * (t % 3) + 256 * (2 - t // 3), COUT), :] = w.astype(F32).T.astype(BF16)
 
     arrived(c_block(cross), cr.at[0])
     send(c_block(cross), c_block(cross), cs.at[2], cr.at[2], (lon, sib))
-    a_of = lax.broadcasted_iota(jnp.int32, (CIN, OWN_IN), 0)
-    b_of = lax.broadcasted_iota(jnp.int32, (CIN, OWN_IN), 1)
-    pick = (a_of == b_of + OWN_IN * rank).astype(F32).astype(BF16)
-    for t in range(16):
-        own_up[t] = nn(up_w[t // 4, t % 4], pick).astype(BF16)
     for n in range(2):
         for d in range(4):
             arrived(ce_all.at[n, lax.rem(rank + 4 - d, 4)], er.at[0, n, d])
@@ -234,8 +225,7 @@
         s = jax.nn.sigmoid(v)
         fs[ts] = s * (1.0 + v * (1.0 - s))
         h = (v * s).astype(BF16).astype(F32).reshape(6, 2, H, COUT)
-        for m, w in enumerate(shifted(h)):
-            hid[m, pl.ds(n * 6, 6)] = w
+        hid[1, pl.ds(n * 6, 6)] = h.reshape(6, 16, COUT).astype(BF16)
 
     pl.loop(0, 11)(activate)
     pass_on(3)
@@ -320,6 +310,15 @@
                 elif ky is (xa, xb)[p % 2]:
                     along_x(ky, p, 0)
 
+    def picked(count, size):
+        row = lax.broadcasted_iota(jnp.int32, (count, size), 0)
+        col = lax.broadcasted_iota(jnp.int32, (count, size), 1)
+        return (row == col + size * rank).astype(F32).astype(BF16)
+
+    pick = picked(CIN, OWN_IN)
+    for t in range(16):
+        own_up[t] = nn(up_w[t // 4, t % 4], pick).astype(BF16)
+
     for d in far_first:
         zz = lax.rem(z + d, nz)
         q = second(zz)
@@ -335,6 +334,17 @@
         total = term if total is None else total + term
     c_pos[...] = total
 
+    pick = picked(COUT, OWN_OUT)
+    for t in range(9):
+        mine[t] = nn(conv_w[t // 3, t % 3], pick).astype(BF16)
+
+    @pl.loop(0, 22)
+    def _(n):
+        v = hid[1, pl.ds(n * 6, 6)].astype(F32).reshape(6, 2, H, COUT)
+        above, _, below = shifted(v)
+        hid[0, pl.ds(n * 6, 6)] = above
+        hid[2, pl.ds(n * 6, 6)] = below
+
     def refine(n):
         acc = None
         for t in range(9):
@@ -342,8 +352,6 @@
             acc = term if acc is None else acc + term
         r_pos[pl.ds(256 * n, 256), :] = acc + own_bias
 
-    for n in range(4):
-        refine(n)
 
     for d in far_first:
         arrived(rx2.at[d], x2r.at[d])
@@ -353,7 +361,7 @@
             send(sb2.at[d], rz.at[d], zs_s.at[d], zs_r.at[d], zdev[d])
         else:
             kept[0] = acc
-    for n in range(4, 8):
+    for n in range(8):
         refine(n)
     acc = kept[0]
     for d in near_first[1:]:

time: 62.8 us -> 63.2 us (level)
  no operation moved by 1% of the time
where the time goes in v8:
time: 63.2 us; the launch traced here: 62.9 us
  Pallas kernels  62.1 us (98%)
  between operations  0.8 us (1%)
    pallas_call x1, Pallas kernels, strip(): pl.pallas_call(functools.partial(kernel, dims), out_shape=(jax.ShapeDtype...  59.5 us
    pallas_call x1, Pallas kernels, unpack(): pl.pallas_call(unpack_kernel, out_shape=(jax.ShapeDtypeStruct(refined.sha...  2.52 us

profile of v8, /device:TPU:2, one launch (start us, length us, event | category | flops | bytes accessed | tf_op | source)
XLA Modules:
  0.0 62.9 jit_solution(16399666086153927021)
XLA Ops:
  0.6 59.5 %strip.1 = (bf16[48,16,128]{2,1,0:T(8,128)(2,1)}, bf16[8,64,96]{2,1,0:T(8,128)(2,1)}, bf16[4,8,96,128]{3,2,1,0:T(8,128)(2,1)}) custom-call(bf16[8,64,96]{2,1,0:T(8,128)(2,1)} %bitcast.7, bf16[48,16,128]{2,1,0:T(8,128)(2,1)} %cot_hbm.1, bf16[4,4,192,384]{3,2,1,0:T(8,128)(2,1)} %bitcast.6, bf16[3,3,192,192]{3,2,1,0:T(8,128)(2,1)} %conv_hbm.1, ...), custom_call_target="tpu_custom_call" | custom-call | tf_op jit(solution)/shard_map/strip/pallas_call | solution.py:424
  60.2 2.5 %unpack.1 = (bf16[48,16,128]{2,1,0:T(8,128)(2,1)}, bf16[8,64,96]{2,1,0:T(8,128)(2,1)}, f32[4,4,96,192]{3,2,1,0:T(8,128)}, f32[3,3,48,192]{3,2,1,0:T(8,128)}) custom-call(bf16[48,16,128]{2,1,0:T(8,128)(2,1)} %get-tuple-element.11.refined, bf16[8,64,96]{2,1,0:T(8,128)(2,1)} %get-tuple-element.12.c_grad, bf16[4,8,96,128]{3,2,1,0:T(8,128)(2,1)} %get-tuple-element.13.sums), custom_call_target="tpu_custom_call" | custom-call | tf_op jit(solution)/shard_map/unpack/pallas_call | solution.py:523

commit v9 on v8

--- a/solution.py
+++ b/solution.py
@@ -44,12 +44,12 @@
     return [jnp.concatenate(pair, 1).astype(BF16) for pair in pairs]
 
 
-def kernel(dims, coarse_hbm, cot_hbm, up_hbm, conv_hbm, up_b, conv_b,
+def kernel(dims, coarse_hbm, cot_hbm, up_hbm, conv_hbm, up_b_hbm, conv_b_hbm,
            refined, c_grad, res,
-           coarse_in, cot_in, coarse, cot, cot3, c_end, g_end, g32, c_all, g_all, ce_all, ge_all, up_w, conv_w, conv_t, mine, own_up,
+           up_b, conv_b, coarse_in, cot_in, coarse, cot, cot3, c_end, g_end, g32, c_all, g_all, ce_all, ge_all, up_w, conv_w, conv_t, mine, own_up,
            xf, xl, pre, fs, hid, cots, df, part, r_pos, c_pos,
-           rx1, kept, sb1, rx2, sb2, rz, ys, yr,
-           w_sem, cs, cr, gs, gr, es, er, x1s, x1r, x2s, x2r, zs_s, zs_r, y_sem,
+           rx1, kept, sb2, rz, ys, yr,
+           w_sem, cs, cr, gs, gr, es, er, x1s, x1r, zs_s, zs_r, y_sem,
            azs, azr, axs, axr):
     nx, nz, ny = dims
     lon, rank = lax.axis_index("lon"), lax.axis_index("chan")
@@ -81,6 +81,8 @@
         pltpu.make_async_copy(cot_hbm, cot_in, w_sem.at[1]),
         pltpu.make_async_copy(up_hbm, up_w, w_sem.at[2]),
         pltpu.make_async_copy(conv_hbm, conv_w, w_sem.at[3]),
+        pltpu.make_async_copy(up_b_hbm, up_b, w_sem.at[4]),
+        pltpu.make_async_copy(conv_b_hbm, conv_b, w_sem.at[5]),
     ]
     for load in loads:
         load.start()
@@ -231,9 +233,11 @@
     pass_on(3)
     pl.loop(11, 22)(activate)
 
-    def along_x(chunk, p, which):
-        send(part.at[chunk, p], rx1.at[p, which], x1s.at[p, which], x1r.at[p, which],
-             dev(first(p), z, y))
+    peers = (xa, xb, xo)
+
+    def along_x(p, which):
+        send(part.at[peers[which], p], rx1.at[p, which], x1s.at[p, which], x1r.at[p, which],
+             dev(peers[which], z, y))
 
     def spot(b):
         return b // 4, 6 + b % 4 // 2, pl.ds(b % 2 * OWN_OUT, OWN_OUT)
@@ -254,8 +258,8 @@
     for b in (14, 15):
         put(b, jnp.zeros((OWN_OUT, 128), F32))
     for p in (6, 7):
-        along_x(xo, p, 1)
-        along_x(first(p), p, 0)
+        for which in (2, 0, 1):
+            along_x(p, which)
 
     def place_cot(at, v, n):
         for m, w in enumerate(shifted(v.reshape(n, 2, H, COUT))):
@@ -298,17 +302,16 @@
     def window(ky, kx):
         return df[kx % 2, ky, pl.ds(kx // 2, 64)].reshape(POS, COUT).astype(BF16)
 
-    for ky in (xo, xa, xb, x):
+    for which in (2, 0, 1, 3):
+        ky = (xa, xb, xo, x)[which]
         for pair in range(2):
             a, b = [nn(coarse[...], window(ky, kx)) for kx in (2 * pair, 2 * pair + 1)]
             slabs = (a[:, :128], jnp.concatenate([a[:, 128:], b[:, :64]], 1), b[:, 64:])
             for n, slab in enumerate(slabs):
                 p = 3 * pair + n
                 part[ky, p] = slab.astype(BF16)
-                if ky is xo:
-                    along_x(xo, p, 1)
-                elif ky is (xa, xb)[p % 2]:
-                    along_x(ky, p, 0)
+                if which < 3:
+                    along_x(p, which)
 
     def picked(count, size):
         row = lax.broadcasted_iota(jnp.int32, (count, size), 0)
@@ -318,15 +321,6 @@
     pick = picked(CIN, OWN_IN)
     for t in range(16):
         own_up[t] = nn(up_w[t // 4, t % 4], pick).astype(BF16)
-
-    for d in far_first:
-        zz = lax.rem(z + d, nz)
-        q = second(zz)
-        for which in range(2):
-            arrived(rx1.at[zz, which], x1r.at[zz, which])
-        kept[d] = part[x, zz].astype(F32) + rx1[zz, 0].astype(F32)
-        sb1[d] = (part[q, zz].astype(F32) + rx1[zz, 1].astype(F32)).astype(BF16)
-        send(sb1.at[d], rx2.at[d], x2s.at[d], x2r.at[d], dev(q, z, y))
 
     total = None
     for t in range(16):
@@ -354,16 +348,19 @@
 
 
     for d in far_first:
-        arrived(rx2.at[d], x2r.at[d])
-        acc = kept[d] + rx2[d].astype(F32)
+        zz = lax.rem(z + d, nz)
+        acc = part[x, zz].astype(F32)
+        for which in range(3):
+            arrived(rx1.at[zz, which], x1r.at[zz, which])
+            acc = acc + rx1[zz, which].astype(F32)
         if d > 0:
             sb2[d] = acc.astype(BF16)
             send(sb2.at[d], rz.at[d], zs_s.at[d], zs_r.at[d], zdev[d])
         else:
-            kept[0] = acc
+            kept[...] = acc
     for n in range(8):
         refine(n)
-    acc = kept[0]
+    acc = kept[...]
     for d in near_first[1:]:
         arrived(rz.at[d], zs_r.at[d])
         acc = acc + rz[d].astype(F32)
@@ -428,9 +425,11 @@
             jax.ShapeDtypeStruct((H, WC, OWN_IN), BF16),
             jax.ShapeDtypeStruct((nx, nz, PIECE, 128), BF16),
         ),
-        in_specs=[any_] * 4 + [VM] * 2,
+        in_specs=[any_] * 6,
         out_specs=[VM] * 3,
         scratch_shapes=[
+            vm((1, COUT), F32),
+            vm((1, COUT), F32),
             vm((H, WC, OWN_IN), BF16),
             vm((OWN_OUT, 2 * H, 2 * WC), BF16),
             vm((OWN_IN, POS), BF16),
@@ -458,16 +457,14 @@
             vm((nx, nz, PIECE, 128), BF16),
             vm((FINE, OWN_OUT), F32),
             vm((POS, OWN_IN), F32),
-            vm((nz, 2, PIECE, 128), BF16),
-            vm((nz, PIECE, 128), F32),
-            vm((nz, PIECE, 128), BF16),
-            vm((nz, PIECE, 128), BF16),
+            vm((nz, 3, PIECE, 128), BF16),
+            vm((PIECE, 128), F32),
             vm((nz, PIECE, 128), BF16),
             vm((nz, PIECE, 128), BF16),
             vm((PIECE, 128), F32),
             vm((PIECE, 128), F32),
-            dma((4,)), dma((3,)), dma((3,)), dma((3, PIECES)), dma((3, PIECES)), dma((2, 2, 4)), dma((2, 2, 4)),
-            dma((nz, 2)), dma((nz, 2)), dma((nz,)), dma((nz,)), dma((nz,)), dma((nz,)), dma((2,)),
+            dma((6,)), dma((3,)), dma((3,)), dma((3, PIECES)), dma((3, PIECES)), dma((2, 2, 4)), dma((2, 2, 4)),
+            dma((nz, 3)), dma((nz, 3)), dma((nz,)), dma((nz,)), dma((2,)),
             dma((nz,)), dma((nz,)), dma((3, nz)), dma((3, nz)),
         ],
         compiler_params=pltpu.CompilerParams(

time: 63.2 us -> 63 us (level)
  no operation moved by 1% of the time
where the time goes in v9:
time: 63 us; the launch traced here: 62.8 us
  Pallas kernels  62 us (98%)
  between operations  0.8 us (1%)
    pallas_call x1, Pallas kernels, strip(): pl.pallas_call(functools.partial(kernel, dims), out_shape=(jax.ShapeDtype...  59.5 us
    pallas_call x1, Pallas kernels, unpack(): pl.pallas_call(unpack_kernel, out_shape=(jax.ShapeDtypeStruct(refined.sha...  2.52 us

profile of v9, /device:TPU:2, one launch (start us, length us, event | category | flops | bytes accessed | tf_op | source)
XLA Modules:
  0.0 62.8 jit_solution(8336872739140501656)
XLA Ops:
  0.6 59.5 %strip.1 = (bf16[48,16,128]{2,1,0:T(8,128)(2,1)}, bf16[8,64,96]{2,1,0:T(8,128)(2,1)}, bf16[4,8,96,128]{3,2,1,0:T(8,128)(2,1)}) custom-call(bf16[8,64,96]{2,1,0:T(8,128)(2,1)} %bitcast.7, bf16[48,16,128]{2,1,0:T(8,128)(2,1)} %cot_hbm.1, bf16[4,4,192,384]{3,2,1,0:T(8,128)(2,1)} %bitcast.6, bf16[3,3,192,192]{3,2,1,0:T(8,128)(2,1)} %conv_hbm.1, ...), custom_call_target="tpu_custom_call" | custom-call | tf_op jit(solution)/shard_map/strip/pallas_call | solution.py:421
  60.2 2.5 %unpack.1 = (bf16[48,16,128]{2,1,0:T(8,128)(2,1)}, bf16[8,64,96]{2,1,0:T(8,128)(2,1)}, f32[4,4,96,192]{3,2,1,0:T(8,128)}, f32[3,3,48,192]{3,2,1,0:T(8,128)}) custom-call(bf16[48,16,128]{2,1,0:T(8,128)(2,1)} %get-tuple-element.11.refined, bf16[8,64,96]{2,1,0:T(8,128)(2,1)} %get-tuple-element.12.c_grad, bf16[4,8,96,128]{3,2,1,0:T(8,128)(2,1)} %get-tuple-element.13.sums), custom_call_target="tpu_custom_call" | custom-call | tf_op jit(solution)/shard_map/unpack/pallas_call | solution.py:520

commit v10 on v9

--- a/solution.py
+++ b/solution.py
@@ -102,37 +102,6 @@
         coarse[:, pl.ds(128 * n, 128)] = c_pos[pl.ds(128 * n, 128), :].T.astype(BF16)
     c_end[0] = c_pos[pl.ds(POS - 16, 16), :].astype(BF16)
     c_end[1] = c_pos[pl.ds(0, 16), :].astype(BF16)
-    pl.semaphore_wait(barrier, len(greet))
-
-    started = []
-
-    def copy_of(a, b, s, r, to):
-        return pltpu.make_async_remote_copy(
-            src_ref=a, dst_ref=b, send_sem=s, recv_sem=r, device_id=to, device_id_type=MESH
-        )
-
-    def send(a, b, s, r, to):
-        copy = copy_of(a, b, s, r, to)
-        copy.start()
-        started.append(copy)
-
-    def arrived(b, r):
-        copy_of(b, b, r, r, (lon, sib)).wait_recv()
-
-    def c_block(r):
-        return c_all.at[pl.ds(pl.multiple_of(r * OWN_IN, 16), OWN_IN), :]
-
-    width = FINE // PIECES
-
-    def g_block(r, k):
-        return g_all.at[pl.ds(pl.multiple_of(r * OWN_OUT, 16), OWN_OUT), pl.ds(k * width, width)]
-
-    send(coarse, c_block(rank), cs.at[0], cr.at[0], (lon, cross))
-    for n, side in enumerate(sides):
-        for d in range(4):
-            to = (side, lax.rem(rank + d, 4))
-            send(c_end.at[n], ce_all.at[n, rank], es.at[0, n, d], er.at[0, n, d], to)
-    send(coarse, c_block(rank), cs.at[1], cr.at[1], (lon, sib))
     loads[1].wait()
     g32[...] = cot_in[...].astype(F32).reshape(OWN_OUT * 16, 128)
     for r in range(2):
@@ -144,6 +113,43 @@
     for n, at in enumerate((FINE - 32, 0)):
         two = [r_pos[pl.ds(at, 16), :], gap, r_pos[pl.ds(at + 16, 16), :], gap]
         g_end[n] = jnp.concatenate(two, 1).astype(BF16)
+    pl.semaphore_wait(barrier, len(greet))
+
+    started = []
+
+    def copy_of(a, b, s, r, to):
+        return pltpu.make_async_remote_copy(
+            src_ref=a, dst_ref=b, send_sem=s, recv_sem=r, device_id=to, device_id_type=MESH
+        )
+
+    def send(a, b, s, r, to):
+        copy = copy_of(a, b, s, r, to)
+        copy.start()
+        started.append(copy)
+
+    def arrived(b, r):
+        copy_of(b, b, r, r, (lon, sib)).wait_recv()
+
+    c_width = POS // 2
+
+    def c_block(r, k):
+        rows = pl.ds(pl.multiple_of(r * OWN_IN, 16), OWN_IN)
+        return c_all.at[rows, pl.ds(k * c_width, c_width)]
+
+    width = FINE // PIECES
+
+    def g_block(r, k):
+        return g_all.at[pl.ds(pl.multiple_of(r * OWN_OUT, 16), OWN_OUT), pl.ds(k * width, width)]
+
+    c_own = [coarse.at[:, pl.ds(k * c_width, c_width)] for k in range(2)]
+    for k in range(2):
+        send(c_own[k], c_block(rank, k), cs.at[0, k], cr.at[0, k], (lon, cross))
+    for n, side in enumerate(sides):
+        for d in range(4):
+            to = (side, lax.rem(rank + d, 4))
+            send(c_end.at[n], ce_all.at[n, rank], es.at[0, n, d], er.at[0, n, d], to)
+    for k in range(2):
+        send(c_own[k], c_block(rank, k), cs.at[1, k], cr.at[1, k], (lon, sib))
     for n, side in enumerate(sides):
         for d in range(4):
             to = (side, lax.rem(rank + d, 4))
@@ -185,15 +191,17 @@
         w = conv_w[t // 3, t % 3]
         conv_t[pl.ds(768 * (t % 3) + 256 * (2 - t // 3), COUT), :] = w.astype(F32).T.astype(BF16)
 
-    arrived(c_block(cross), cr.at[0])
-    send(c_block(cross), c_block(cross), cs.at[2], cr.at[2], (lon, sib))
+    for k in range(2):
+        arrived(c_block(cross, k), cr.at[0, k])
+        send(c_block(cross, k), c_block(cross, k), cs.at[2, k], cr.at[2, k], (lon, sib))
+    for k in range(2):
+        arrived(c_block(sib, k), cr.at[1, k])
+        arrived(c_block(diag, k), cr.at[2, k])
+        for b in (2 * k, 2 * k + 1):
+            xf[pl.ds(1 + 16 * b, 16)] = c_all[:, pl.ds(128 * b, 128)].astype(F32).T.reshape(16, H, CIN)
     for n in range(2):
         for d in range(4):
             arrived(ce_all.at[n, lax.rem(rank + 4 - d, 4)], er.at[0, n, d])
-    arrived(c_block(sib), cr.at[1])
-    arrived(c_block(diag), cr.at[2])
-    for b in range(4):
-        xf[pl.ds(1 + 16 * b, 16)] = c_all[:, pl.ds(128 * b, 128)].astype(F32).T.reshape(16, H, CIN)
     left, right = [
         jnp.concatenate([ce_all[n, r].astype(F32) for r in range(4)], 1) for n in range(2)
     ]
@@ -463,7 +471,7 @@
             vm((nz, PIECE, 128), BF16),
             vm((PIECE, 128), F32),
             vm((PIECE, 128), F32),
-            dma((6,)), dma((3,)), dma((3,)), dma((3, PIECES)), dma((3, PIECES)), dma((2, 2, 4)), dma((2, 2, 4)),
+            dma((6,)), dma((3, 2)), dma((3, 2)), dma((3, PIECES)), dma((3, PIECES)), dma((2, 2, 4)), dma((2, 2, 4)),
             dma((nz, 3)), dma((nz, 3)), dma((nz,)), dma((nz,)), dma((2,)),
             dma((nz,)), dma((nz,)), dma((3, nz)), dma((3, nz)),
         ],

time: 63 us -> 62.7 us (level)
  no operation moved by 1% of the time
where the time goes in v10:
time: 62.7 us; the launch traced here: 62.5 us
  Pallas kernels  61.7 us (98%)
  between operations  0.8 us (1%)
    pallas_call x1, Pallas kernels, strip(): pl.pallas_call(functools.partial(kernel, dims), out_shape=(jax.ShapeDtype...  59.2 us
    pallas_call x1, Pallas kernels, unpack(): pl.pallas_call(unpack_kernel, out_shape=(jax.ShapeDtypeStruct(refined.sha...  2.52 us

profile of v10, /device:TPU:2, one launch (start us, length us, event | category | flops | bytes accessed | tf_op | source)
XLA Modules:
  0.0 62.5 jit_solution(11480651158084259950)
XLA Ops:
  0.6 59.2 %strip.1 = (bf16[48,16,128]{2,1,0:T(8,128)(2,1)}, bf16[8,64,96]{2,1,0:T(8,128)(2,1)}, bf16[4,8,96,128]{3,2,1,0:T(8,128)(2,1)}) custom-call(bf16[8,64,96]{2,1,0:T(8,128)(2,1)} %bitcast.7, bf16[48,16,128]{2,1,0:T(8,128)(2,1)} %cot_hbm.1, bf16[4,4,192,384]{3,2,1,0:T(8,128)(2,1)} %bitcast.6, bf16[3,3,192,192]{3,2,1,0:T(8,128)(2,1)} %conv_hbm.1, ...), custom_call_target="tpu_custom_call" | custom-call | tf_op jit(solution)/shard_map/strip/pallas_call | solution.py:429
  59.9 2.5 %unpack.1 = (bf16[48,16,128]{2,1,0:T(8,128)(2,1)}, bf16[8,64,96]{2,1,0:T(8,128)(2,1)}, f32[4,4,96,192]{3,2,1,0:T(8,128)}, f32[3,3,48,192]{3,2,1,0:T(8,128)}) custom-call(bf16[48,16,128]{2,1,0:T(8,128)(2,1)} %get-tuple-element.11.refined, bf16[8,64,96]{2,1,0:T(8,128)(2,1)} %get-tuple-element.12.c_grad, bf16[4,8,96,128]{3,2,1,0:T(8,128)(2,1)} %get-tuple-element.13.sums), custom_call_target="tpu_custom_call" | custom-call | tf_op jit(solution)/shard_map/unpack/pallas_call | solution.py:528

commit v11 on v10

--- a/solution.py
+++ b/solution.py
@@ -14,7 +14,7 @@
 OWN_IN, OWN_OUT = CIN // 4, COUT // 4
 POS, FINE = H * WC, 4 * H * WC
 PIECE = 96
-LIMIT = 60 << 20
+LIMIT = 52 << 20
 
 
 def nn(a, b):
@@ -425,7 +425,7 @@
     nx, nz, ny = dims
     dma = pltpu.SemaphoreType.DMA
     vm = pltpu.VMEM
-    any_ = pl.BlockSpec(memory_space=pl.ANY)
+    hbm = pl.BlockSpec(memory_space=pltpu.HBM)
     return pl.pallas_call(
         functools.partial(kernel, dims),
         out_shape=(
@@ -433,7 +433,7 @@
             jax.ShapeDtypeStruct((H, WC, OWN_IN), BF16),
             jax.ShapeDtypeStruct((nx, nz, PIECE, 128), BF16),
         ),
-        in_specs=[any_] * 6,
+        in_specs=[hbm] * 6,
         out_specs=[VM] * 3,
         scratch_shapes=[
             vm((1, COUT), F32),
@@ -523,6 +523,7 @@
 
 def unpack(refined, c_grad, sums):
     any_ = pl.BlockSpec(memory_space=pl.ANY)
+    hbm = pl.BlockSpec(memory_space=pltpu.HBM)
     up = (4, 4, OWN_IN, COUT)
     conv = (3, 3, OWN_OUT, COUT)
     return pl.pallas_call(
@@ -534,7 +535,7 @@
             jax.ShapeDtypeStruct(conv, F32),
         ),
         in_specs=[any_] * 3,
-        out_specs=[any_] * 4,
+        out_specs=[hbm] * 4,
         scratch_shapes=[
             pltpu.VMEM(refined.shape, BF16),
             pltpu.VMEM(c_grad.shape, BF16),
@@ -544,7 +545,7 @@
             pltpu.SemaphoreType.DMA((6,)),
             pltpu.SemaphoreType.DMA((7,)),
         ],
-        compiler_params=pltpu.CompilerParams(vmem_limit_bytes=LIMIT),
+        compiler_params=pltpu.CompilerParams(vmem_limit_bytes=12 << 20),
         name="unpack",
     )(refined, c_grad, sums)
 

time: 62.7 us -> 65.1 us (1.038)
  local copies, waits for them, and re-layouts: 0 us -> 3.18 us
  Pallas kernels: 61.7 us -> 60.7 us
    unnamed x0 -> x8, local copies, waits for them, and re-layouts: none -> 3.18 us
    pallas_call x1, Pallas kernels: 59.2 us -> 57.6 us  [strip(): pl.pallas_call(functools.partial(kernel, dims), out_shape=(jax.ShapeDtype...]
where the time goes in v11:
time: 65.1 us; the launch traced here: 64.7 us
  Pallas kernels  60.7 us (93%)
  local copies, waits for them, and re-layouts  3.18 us (5%)
  between operations  0.81 us (1%)
    pallas_call x1, Pallas kernels, strip(): pl.pallas_call(functools.partial(kernel, dims), out_shape=(jax.ShapeDtype...  57.6 us
    unnamed x8, local copies, waits for them, and re-layouts  3.18 us
    pallas_call x1, Pallas kernels, unpack(): pl.pallas_call(unpack_kernel, out_shape=(jax.ShapeDtypeStruct(refined.sha...  3.03 us

profile of v11, /device:TPU:2, one launch (start us, length us, event | category | flops | bytes accessed | tf_op | source)
XLA Modules:
  0.0 64.7 jit_solution(15331246604395069427)
XLA Ops:
  0.6 0.0 copy-start
  0.6 0.9 %copy-done = bf16[48,16,128]{2,1,0:T(8,128)(2,1)S(1)} copy-done((bf16[48,16,128]{2,1,0:T(8,128)(2,1)S(1)}, bf16[48,16,128]{2,1,0:T(8,128)(2,1)}, u32[]{:S(2)}) %copy-start) | copy-done | bytes 196632
  1.6 0.0 copy-start.1
  1.6 0.9 %copy-done.1 = bf16[96,8,64]{0,2,1:T(8,128)(2,1)S(1)} copy-done((bf16[96,8,64]{0,2,1:T(8,128)(2,1)S(1)}, bf16[96,8,64]{0,2,1:T(8,128)(2,1)}, u32[]{:S(2)}) %copy-start.1) | copy-done | bytes 98328
  2.5 0.0 copy-start.2
  2.5 0.7 %copy-done.2 = f32[192]{0:T(256)S(1)} copy-done((f32[192]{0:T(256)S(1)}, f32[192]{0:T(256)}, u32[]{:S(2)}) %copy-start.2) | copy-done | bytes 792
  3.1 0.0 copy-start.3
  3.1 0.7 %copy-done.3 = f32[192]{0:T(256)S(1)} copy-done((f32[192]{0:T(256)S(1)}, f32[192]{0:T(256)}, u32[]{:S(2)}) %copy-start.3) | copy-done | bytes 792
  3.8 57.6 %strip.1 = (bf16[48,16,128]{2,1,0:T(8,128)(2,1)S(1)}, bf16[8,64,96]{2,1,0:T(8,128)(2,1)S(1)}, bf16[4,8,96,128]{3,2,1,0:T(8,128)(2,1)S(1)}) custom-call(bf16[8,64,96]{2,1,0:T(8,128)(2,1)S(1)} %bitcast.6, bf16[48,16,128]{2,1,0:T(8,128)(2,1)S(1)} %copy-done, bf16[4,4,192,384]{3,2,1,0:T(8,128)(2,1)} %bitcast.9, bf16[3,3,192,192]{3,2,1,0:T(8,128)(2,1)} %conv_hbm.1, ...), custom_call_target="tpu_custom_call" | custom-call | tf_op jit(solution)/shard_map/strip/pallas_call | solution.py:429
  61.5 3.0 %unpack.1 = (bf16[48,16,128]{2,1,0:T(8,128)(2,1)}, bf16[8,64,96]{2,1,0:T(8,128)(2,1)}, f32[4,4,96,192]{3,2,1,0:T(8,128)}, f32[3,3,48,192]{3,2,1,0:T(8,128)}) custom-call(bf16[48,16,128]{2,1,0:T(8,128)(2,1)S(1)} %get-tuple-element.11.refined, bf16[8,64,96]{2,1,0:T(8,128)(2,1)S(1)} %get-tuple-element.12.c_grad, bf16[4,8,96,128]{3,2,1,0:T(8,128)(2,1)S(1)} %get-tuple-element.13.sums), custom_call_target="tpu_custom_call" | custom-call | tf_op jit(solution)/shard_map/unpack/pallas_call | solution.py:529
Async XLA Ops:
  0.6 0.9 %copy-start = (bf16[48,16,128]{2,1,0:T(8,128)(2,1)S(1)}, bf16[48,16,128]{2,1,0:T(8,128)(2,1)}, u32[]{:S(2)}) copy-start(bf16[48,16,128]{2,1,0:T(8,128)(2,1)} %cot_hbm.1) | copy-start | bytes 589828
  1.6 0.9 %copy-start.1 = (bf16[96,8,64]{0,2,1:T(8,128)(2,1)S(1)}, bf16[96,8,64]{0,2,1:T(8,128)(2,1)}, u32[]{:S(2)}) copy-start(bf16[96,8,64]{0,2,1:T(8,128)(2,1)} %param.6) | copy-start | bytes 294916
  2.5 0.7 %copy-start.2 = (f32[192]{0:T(256)S(1)}, f32[192]{0:T(256)}, u32[]{:S(2)}) copy-start(f32[192]{0:T(256)} %param.8) | copy-start | bytes 2308
  3.1 0.7 %copy-start.3 = (f32[192]{0:T(256)S(1)}, f32[192]{0:T(256)}, u32[]{:S(2)}) copy-start(f32[192]{0:T(256)} %param.10) | copy-start | bytes 2308

commit v12 on v10

--- a/solution.py
+++ b/solution.py
@@ -237,9 +237,8 @@
         h = (v * s).astype(BF16).astype(F32).reshape(6, 2, H, COUT)
         hid[1, pl.ds(n * 6, 6)] = h.reshape(6, 16, COUT).astype(BF16)
 
-    pl.loop(0, 11)(activate)
     pass_on(3)
-    pl.loop(11, 22)(activate)
+    pl.loop(0, 22)(activate)
 
     peers = (xa, xb, xo)
 
@@ -381,7 +380,7 @@
         send(here, here, azs.at[d], azr.at[d], zdev[d])
 
     def direct(d):
-        return d == nz // 2
+        return min(d, nz - d) >= 3
 
     def spread_x(d):
         zz = lax.rem(z + nz - d, nz)
@@ -400,7 +399,7 @@
         if not direct(d):
             send(got, got, axs.at[2, d], axr.at[2, d], dev(first(zz), z, y))
 
-    lag = 3
+    lag = 4
     for n in range(nz + lag):
         if n < nz:
             spread_x(near_first[n])

time: 62.7 us -> 61.4 us (0.979)
  Pallas kernels: 61.7 us -> 60.5 us
    pallas_call x1, Pallas kernels: 59.2 us -> 58 us  [strip(): pl.pallas_call(functools.partial(kernel, dims), out_shape=(jax.ShapeDtype...]
where the time goes in v12:
time: 61.4 us; the launch traced here: 61.3 us
  Pallas kernels  60.5 us (99%)
  between operations  0.8 us (1%)
    pallas_call x1, Pallas kernels, strip(): pl.pallas_call(functools.partial(kernel, dims), out_shape=(jax.ShapeDtype...  58 us
    pallas_call x1, Pallas kernels, unpack(): pl.pallas_call(unpack_kernel, out_shape=(jax.ShapeDtypeStruct(refined.sha...  2.52 us

profile of v12, /device:TPU:2, one launch (start us, length us, event | category | flops | bytes accessed | tf_op | source)
XLA Modules:
  0.0 61.3 jit_solution(16149601970356131361)
XLA Ops:
  0.6 58.0 %strip.1 = (bf16[48,16,128]{2,1,0:T(8,128)(2,1)}, bf16[8,64,96]{2,1,0:T(8,128)(2,1)}, bf16[4,8,96,128]{3,2,1,0:T(8,128)(2,1)}) custom-call(bf16[8,64,96]{2,1,0:T(8,128)(2,1)} %bitcast.7, bf16[48,16,128]{2,1,0:T(8,128)(2,1)} %cot_hbm.1, bf16[4,4,192,384]{3,2,1,0:T(8,128)(2,1)} %bitcast.6, bf16[3,3,192,192]{3,2,1,0:T(8,128)(2,1)} %conv_hbm.1, ...), custom_call_target="tpu_custom_call" | custom-call | tf_op jit(solution)/shard_map/strip/pallas_call | solution.py:428
  58.6 2.5 %unpack.1 = (bf16[48,16,128]{2,1,0:T(8,128)(2,1)}, bf16[8,64,96]{2,1,0:T(8,128)(2,1)}, f32[4,4,96,192]{3,2,1,0:T(8,128)}, f32[3,3,48,192]{3,2,1,0:T(8,128)}) custom-call(bf16[48,16,128]{2,1,0:T(8,128)(2,1)} %get-tuple-element.11.refined, bf16[8,64,96]{2,1,0:T(8,128)(2,1)} %get-tuple-element.12.c_grad, bf16[4,8,96,128]{3,2,1,0:T(8,128)(2,1)} %get-tuple-element.13.sums), custom_call_target="tpu_custom_call" | custom-call | tf_op jit(solution)/shard_map/unpack/pallas_call | solution.py:527

commit v13 on v12

--- a/solution.py
+++ b/solution.py
@@ -380,7 +380,7 @@
         send(here, here, azs.at[d], azr.at[d], zdev[d])
 
     def direct(d):
-        return min(d, nz - d) >= 3
+        return min(d, nz - d) >= 2
 
     def spread_x(d):
         zz = lax.rem(z + nz - d, nz)

time: 61.4 us -> 61.5 us (level)
  no operation moved by 1% of the time
where the time goes in v13:
time: 61.5 us; the launch traced here: 61.4 us
  Pallas kernels  60.6 us (99%)
  between operations  0.8 us (1%)
    pallas_call x1, Pallas kernels, strip(): pl.pallas_call(functools.partial(kernel, dims), out_shape=(jax.ShapeDtype...  58.1 us
    pallas_call x1, Pallas kernels, unpack(): pl.pallas_call(unpack_kernel, out_shape=(jax.ShapeDtypeStruct(refined.sha...  2.52 us

profile of v13, /device:TPU:2, one launch (start us, length us, event | category | flops | bytes accessed | tf_op | source)
XLA Modules:
  0.0 61.4 jit_solution(8996645845997941493)
XLA Ops:
  0.6 58.1 %strip.1 = (bf16[48,16,128]{2,1,0:T(8,128)(2,1)}, bf16[8,64,96]{2,1,0:T(8,128)(2,1)}, bf16[4,8,96,128]{3,2,1,0:T(8,128)(2,1)}) custom-call(bf16[8,64,96]{2,1,0:T(8,128)(2,1)} %bitcast.7, bf16[48,16,128]{2,1,0:T(8,128)(2,1)} %cot_hbm.1, bf16[4,4,192,384]{3,2,1,0:T(8,128)(2,1)} %bitcast.6, bf16[3,3,192,192]{3,2,1,0:T(8,128)(2,1)} %conv_hbm.1, ...), custom_call_target="tpu_custom_call" | custom-call | tf_op jit(solution)/shard_map/strip/pallas_call | solution.py:428
  58.7 2.5 %unpack.1 = (bf16[48,16,128]{2,1,0:T(8,128)(2,1)}, bf16[8,64,96]{2,1,0:T(8,128)(2,1)}, f32[4,4,96,192]{3,2,1,0:T(8,128)}, f32[3,3,48,192]{3,2,1,0:T(8,128)}) custom-call(bf16[48,16,128]{2,1,0:T(8,128)(2,1)} %get-tuple-element.11.refined, bf16[8,64,96]{2,1,0:T(8,128)(2,1)} %get-tuple-element.12.c_grad, bf16[4,8,96,128]{3,2,1,0:T(8,128)(2,1)} %get-tuple-element.13.sums), custom_call_target="tpu_custom_call" | custom-call | tf_op jit(solution)/shard_map/unpack/pallas_call | solution.py:527
